TPU v7x, 32 devices: a whole 2x2x4 slice. The times are simulated.
32 devices in a mesh: layer: 8 (over y, x, core), feat: 4 (over z).
Axes of the slice: x: 2, y: 2, z: 4, core: 2. Of those that a mesh axis runs over, the one named last changes fastest.
Arguments:
- latents: bfloat16 [2048, 16384], P('layer', 'feat'), may hold values from 0.5 to 3
- block_lists: int32 [4, 16, 64], replicated, may hold values from 0 to 127, all different within a row
- decoders: bfloat16 [2, 16384, 32768], P(None, 'feat', 'layer'), may hold values from -0.03125 to 0.03125
- targets: bfloat16 [512, 32768], P('feat', 'layer'), may hold values from -6 to 6
Outputs:
- errors: bfloat16 [512, 32768], P('feat', 'layer')
- latent_grad: float32 [2048, 16384], P('layer', 'feat')
Inputs may be any that keep to these rules, and one draw needn't show every extreme that they name: `block_lists`: each row names 64 different latent blocks, and every block is named by some row.
All inputs are finite; a program needn't handle non-finite values.
Results may differ from a plain program's by a relative error of at most 0.006.
Values may be sent and summed in bfloat16 or wider, within the bound.
A program may use at most 192 MiB of HBM per device.

v0:
```python
import jax
import jax.numpy as jnp
from jax import lax
from jax.sharding import PartitionSpec as P

D = 8192
BLOCK = 128


def swapped(value, axis, bit):
    mask = 2**bit
    pairs = [(source, source ^ mask) for source in range(lax.axis_size(axis))]
    return lax.ppermute(value, axis, pairs)


def passed_along(value, axis, steps):
    count = lax.axis_size(axis)
    first, last = (max(0, -steps), min(count, count - steps))
    return lax.ppermute(value, axis, [(source, source + steps) for source in range(first, last)])


def doubled(held_rows, partner_rows, upper_half):
    return jnp.where(
        upper_half,
        jnp.concatenate([partner_rows, held_rows], 0),
        jnp.concatenate([held_rows, partner_rows], 0),
    )


def pick_half(block, upper_half, axis):
    half_rows = block.shape[axis] // 2
    lower = lax.slice_in_dim(block, 0, half_rows, axis=axis)
    higher = lax.slice_in_dim(block, half_rows, 2 * half_rows, axis=axis)
    return (jnp.where(upper_half, higher, lower), jnp.where(upper_half, lower, higher))


def local(latents, block_lists, decoders, targets):
    layer_pos = lax.axis_index("layer")
    feat_pos = lax.axis_index("feat")
    width_cols = decoders.shape[2]
    groups = D // width_cols
    width_bits = groups.bit_length() - 1
    layer_id = layer_pos // groups
    member = layer_pos % groups
    quarter, feat_cols = latents.shape
    total_rows = quarter * groups
    block_rows = total_rows // block_lists.shape[1]
    blocks_here = feat_cols // BLOCK
    lists = lax.dynamic_index_in_dim(block_lists, layer_id, 0, keepdims=False)
    wanted = feat_pos * blocks_here + jnp.arange(blocks_here, dtype=jnp.int32)
    hit = jnp.any(lists[:, :, None] == wanted[None, None, :], axis=1)
    row_hit = jnp.repeat(hit, block_rows, axis=0)
    row_hit = lax.dynamic_slice_in_dim(row_hit, member * quarter, quarter, 0)
    tile_mask = jnp.repeat(row_hit, BLOCK, axis=1)
    own_tile = jnp.where(tile_mask, latents, jnp.zeros_like(latents))
    own_all = own_tile
    for bit_pos in range(width_bits):
        upper_half = member // (1 << bit_pos) % 2 == 1
        partner_rows = swapped(own_all, "layer", bit_pos)
        own_all = doubled(own_all, partner_rows, upper_half)
    prior_all = passed_along(own_all, "layer", groups)
    summed = jnp.dot(own_all, decoders[0], preferred_element_type=jnp.float32)
    recon_rows = lax.psum_scatter(
        summed + jnp.dot(prior_all, decoders[1], preferred_element_type=jnp.float32),
        "feat",
        scatter_dimension=0,
        tiled=True,
    )
    errors_here = (recon_rows - targets.astype(jnp.float32)).astype(jnp.bfloat16)
    grad_terms = jnp.einsum(
        "tc,kfc->ktf",
        lax.all_gather(errors_here, "feat", axis=0, tiled=True),
        decoders,
        preferred_element_type=jnp.float32,
    )
    grad_pair = grad_terms
    for bit_pos in reversed(range(width_bits)):
        upper_half = member // (1 << bit_pos) % 2 == 1
        kept_part, sent_part = pick_half(grad_pair, upper_half, 1)
        grad_pair = kept_part + swapped(sent_part.astype(jnp.bfloat16), "layer", bit_pos).astype(
            sent_part.dtype
        )
    from_next = passed_along(grad_pair[1].astype(jnp.bfloat16), "layer", -groups).astype(
        jnp.float32
    )
    combined = grad_pair[0] + from_next
    latent_grad = jnp.where(tile_mask, combined, jnp.zeros_like(combined))
    return (errors_here, latent_grad)


def solution(mesh):
    placed = (P("layer", "feat"), P(), P(None, "feat", "layer"), P("feat", "layer"))
    return jax.shard_map(
        local,
        mesh=mesh,
        in_specs=placed,
        out_specs=(P("feat", "layer"), P("layer", "feat")),
        check_vma=False,
    )
```

profile of v0, /device:TPU:0, one launch (start us, length us, event | category | flops | bytes accessed | tf_op | source)
XLA Modules:
  0.0 514.2 jit_solution(1743525164751102454)
XLA Ops:
  7.3 0.7 copy-done
  7.9 0.4 compare_reduce_fusion
  8.4 2.1 broadcast_in_dim.15
  10.5 2.2 bitcast_select_fusion
  12.7 0.5 collective-permute-start
  13.2 3.9 collective-permute-done
  17.1 3.3 maximum_select_fusion
  20.4 5.0 collective-permute-start.1
  25.4 89.8 %collective-permute-done.1 = bf16[512,4096]{1,0:T(8,128)(2,1)S(1)} collective-permute-done((bf16[512,4096]{1,0:T(8,128)(2,1)S(1)}, bf16[512,4096]{1,0:T(8,128)(2,1)S(1)}, u32[]{:S(2)}, u32[]{:S(2)}) %collective-permute-start.1) | collective-permute-done | bytes 4194336 | tf_op jit(solution)/shard_map/ppermute | solution.py:19
  115.3 21.7 %fusion = f32[512,4096]{1,0:T(8,128)S(1)} fusion(bf16[512,4096]{1,0:T(8,128)(2,1)S(1)} %collective-permute-done.1, bf16[2,4096,4096]{2,1,0:T(8,128)(2,1)} %param.6), kind=kOutput, calls=%fused_computation | convolution fusion | flops 17179869184 | bytes 46137344 | tf_op jit(solution)/shard_map/dot_general | solution.py:64
  137.0 23.1 %fusion.6 = f32[512,4096]{1,0:T(8,128)} fusion(f32[512,4096]{1,0:T(8,128)S(1)} %fusion, bf16[512,4096]{1,0:T(8,128)(2,1)S(1)} %maximum_select_fusion, bf16[2,4096,4096]{2,1,0:T(8,128)(2,1)} %param.6), kind=kOutput, calls=%fused_computation.9 | convolution fusion | flops 17181966336 | bytes 54525952 | tf_op jit(solution)/shard_map/dot_general | solution.py:62
  160.1 0.2 all-gather.2.cloned.1.call-start
  160.3 146.6 %reduce-scatter.2.cloned.1.call-done = f32[128,4096]{1,0:T(8,128)} async-done(((f32[512,4096]{1,0:T(8,128)}), f32[128,4096]{1,0:T(8,128)}) %reduce-scatter.2.cloned.1.call-update) | async-done | bytes 2097168 | tf_op jit(solution)/shard_map/reduce_scatter | solution.py:63
  306.9 2.8 subtract_convert_fusion
  309.7 81.6 %all-gather.2.cloned.1.call-done = bf16[512,4096]{1,0:T(8,128)(2,1)} async-done(((bf16[128,4096]{1,0:T(8,128)(2,1)}), bf16[512,4096]{1,0:T(8,128)(2,1)}) %all-gather.2.cloned.1.call-update) | async-done | bytes 4194320 | tf_op jit(solution)/shard_map/all_gather | solution.py:72
  391.4 42.2 %convolution_bitcast_fusion = f32[2,512,4096]{2,1,0:T(8,128)} fusion(bf16[2,4096,4096]{2,1,0:T(8,128)(2,1)} %param.6, bf16[512,4096]{1,0:T(8,128)(2,1)} %all-gather.2.cloned.1.call-done), kind=kOutput, calls=%fused_computation.6 | convolution fusion | flops 34359738368 | bytes 88080384 | tf_op jit(solution)/shard_map/tc,kfc->ktf/dot_general | solution.py:70
  433.6 6.2 %select_convert_fusion = bf16[2,256,4096]{2,1,0:T(8,128)(2,1)S(1)} fusion(f32[2,512,4096]{2,1,0:T(8,128)} %convolution_bitcast_fusion, pred[]{:T(512)S(6)} %eq.23), kind=kLoop, calls=%fused_computation.8 | loop fusion | flops 2097152 | bytes 12582913 | tf_op jit(solution)/shard_map/convert_element_type | solution.py:80
  439.8 0.1 collective-permute-start.2
  439.9 7.1 %collective-permute-done.2 = bf16[2,256,4096]{2,1,0:T(8,128)(2,1)S(1)} collective-permute-done((bf16[2,256,4096]{2,1,0:T(8,128)(2,1)S(1)}, bf16[2,256,4096]{2,1,0:T(8,128)(2,1)S(1)}, u32[]{:S(2)}, u32[]{:S(2)}) %collective-permute-start.2) | collective-permute-done | bytes 4194336 | tf_op jit(solution)/shard_map/ppermute | solution.py:13
  447.1 7.1 %convert_add_fusion = f32[2,256,4096]{2,1,0:T(8,128)S(1)} fusion(bf16[2,256,4096]{2,1,0:T(8,128)(2,1)S(1)} %collective-permute-done.2, f32[2,512,4096]{2,1,0:T(8,128)} %convolution_bitcast_fusion, pred[]{:T(512)S(6)} %eq.23), kind=kLoop, calls=%fused_computation.7 | loop fusion | flops 6291456 | bytes 29360128 | tf_op jit(solution)/shard_map/add | solution.py:80
  454.2 0.3 fusion.12
  454.5 1.3 collective-permute-start.3
  455.8 48.3 %collective-permute-done.3 = bf16[256,4096]{1,0:T(8,128)(2,1)S(1)} collective-permute-done((bf16[256,4096]{1,0:T(8,128)(2,1)S(1)}, bf16[256,4096]{1,0:T(8,128)(2,1)S(1)}, u32[]{:S(2)}, u32[]{:S(2)}) %collective-permute-start.3) | collective-permute-done | bytes 2097184 | tf_op jit(solution)/shard_map/ppermute | solution.py:19
  504.0 3.3 fusion.10
  (12 shorter events, 0.1 us)
Async XLA Ops:
  7.2 0.8 copy-start
  7.2 299.7 %reduce-scatter.2.cloned.1.call-start = ((), (), s32[]{:S(2)}) async-start(), calls=%async_computation.1 | async-start | bytes 10485760 | tf_op jit(solution)/shard_map/reduce_scatter | solution.py:63
  12.7 4.4 collective-permute-start
  20.4 94.9 %collective-permute-start.1 = (bf16[512,4096]{1,0:T(8,128)(2,1)S(1)}, bf16[512,4096]{1,0:T(8,128)(2,1)S(1)}, u32[]{:S(2)}, u32[]{:S(2)}) collective-permute-start(bf16[512,4096]{1,0:T(8,128)(2,1)S(1)} %maximum_select_fusion), channel_id=1, source_target_pairs={{0,8},{4,12},{8,16},{12,20},{16,24},{20,28},{1,9},{5,13},{9,17},{1... | collective-permute-start | bytes 12582920 | tf_op jit(solution)/shard_map/ppermute | solution.py:19
  160.0 146.9 %copy-start.2 = (bf16[128,4096]{1,0:T(8,128)(2,1)S(1)}, bf16[128,4096]{1,0:T(8,128)(2,1)}, u32[]{:S(2)}) copy-start(bf16[128,4096]{1,0:T(8,128)(2,1)} %param.7) | copy-start | bytes 3145732
  160.1 231.3 %all-gather.2.cloned.1.call-start = ((), (), s32[]{:S(2)}) async-start(), calls=%async_computation.2 | async-start | bytes 5242880 | tf_op jit(solution)/shard_map/all_gather | solution.py:72
  439.8 7.2 %collective-permute-start.2 = (bf16[2,256,4096]{2,1,0:T(8,128)(2,1)S(1)}, bf16[2,256,4096]{2,1,0:T(8,128)(2,1)S(1)}, u32[]{:S(2)}, u32[]{:S(2)}) collective-permute-start(bf16[2,256,4096]{2,1,0:T(8,128)(2,1)S(1)} %select_convert_fusion), channel_id=1, source_target_pairs={{0,4},{4,0},{8,12},{12,8},{16,20},{20,16},{24,28},{28,24},{1,5},{5... | collective-permute-start | bytes 12582920 | tf_op jit(solution)/shard_map/ppermute | solution.py:13
  454.2 53.2 %copy-start.1 = (s32[4,16,64]{2,1,0:T(8,128)S(1)}, s32[4,16,64]{2,1,0:T(8,128)}, u32[]{:S(2)}) copy-start(s32[4,16,64]{2,1,0:T(8,128)} %param.5) | copy-start | bytes 49156
  454.5 49.6 %collective-permute-start.3 = (bf16[256,4096]{1,0:T(8,128)(2,1)S(1)}, bf16[256,4096]{1,0:T(8,128)(2,1)S(1)}, u32[]{:S(2)}, u32[]{:S(2)}) collective-permute-start(bf16[256,4096]{1,0:T(8,128)(2,1)S(1)} %fusion.12), channel_id=1, source_target_pairs={{8,0},{12,4},{16,8},{20,12},{24,16},{28,20},{9,1},{13,5},{17,9},{2... | collective-permute-start | bytes 6291464 | tf_op jit(solution)/shard_map/ppermute | solution.py:19
Sparse Core Ops, SparseCore 0:
  160.2 146.6 reduce-scatter.1
  309.8 81.4 all-gather.1
where the time goes:
time: 515 us; the launch traced here: 514 us
  waiting for transfers between devices  377 us (73%)
  matrix products  87 us (17%)
  other arithmetic  25.3 us (5%)
  between operations  14.2 us (3%)
  starting transfers between devices  7.17 us (1%)
    reduce_scatter x1, waiting for transfers between devices, local(): lax.psum_scatter(summed + jnp.dot(prior_all, decoders[1], preferred_eleme...  147 us
    ppermute x2, waiting for transfers between devices, passed_along(): lax.ppermute(value, axis, [(source, source + steps) for source in range(f...  138 us
    all_gather x1, waiting for transfers between devices, local(): lax.all_gather(errors_here, 'feat', axis=0, tiled=True)  81.6 us
    dot_general x1, matrix products, local(): jnp.einsum('tc,kfc->ktf', lax.all_gather(errors_here, 'feat', axis=0, til...  42.2 us
    dot_general x1, matrix products, local(): summed = jnp.dot(own_all, decoders[0], preferred_element_type=jnp.float32)  23.1 us
    dot_general x1, matrix products, local(): jnp.dot(prior_all, decoders[1], preferred_element_type=jnp.float32)  21.7 us
    ppermute x2, waiting for transfers between devices, swapped(): return lax.ppermute(value, axis, pairs)  11.1 us
  transfers between devices with their start and end apart: 6, of which 6 were waited for; matrix products, arithmetic and copies ran while one was open for 0% of the time, Pallas kernels for 0%

commit v1 on v0

--- a/solution.py
+++ b/solution.py
@@ -5,6 +5,8 @@
 
 D = 8192
 BLOCK = 128
+CHUNKS = 8
+PARTS = 4
 
 
 def swapped(value, axis, bit):
@@ -88,10 +90,170 @@
     return (errors_here, latent_grad)
 
 
+def tied(*values):
+    return lax.optimization_barrier(values)
+
+
+def chain_local(latents, block_lists, decoders, targets):
+    layer_pos = lax.axis_index("layer")
+    feat_pos = lax.axis_index("feat")
+    width_cols = decoders.shape[2]
+    layer_id = layer_pos // 2
+    member = layer_pos % 2
+    held_rows, feat_cols = latents.shape
+    half_rows = held_rows // 2
+    tok_blocks = block_lists.shape[1]
+    block_rows = 2 * held_rows // tok_blocks
+    blocks_here = feat_cols // BLOCK
+
+    raw_before = [
+        passed_along(latents[half * half_rows : (half + 1) * half_rows], "layer", 2)
+        for half in range(2)
+    ]
+    raw_partner = swapped(latents, "layer", 0)
+
+    wanted = feat_pos * blocks_here + jnp.arange(blocks_here, dtype=jnp.int32)
+
+    def masked(rows, layer, owner, start):
+        lists = lax.dynamic_index_in_dim(block_lists, layer, 0, keepdims=False)
+        hit = jnp.any(lists[:, :, None] == wanted[None, None, :], axis=1)
+        count = rows.shape[0] // block_rows
+        first = owner * (tok_blocks // 2) + start // block_rows
+        hit = lax.dynamic_slice_in_dim(hit, first, count, 0)
+        tile_mask = jnp.repeat(jnp.repeat(hit, block_rows, axis=0), BLOCK, axis=1)
+        return jnp.where(tile_mask, rows, jnp.zeros_like(rows))
+
+    own_all = jnp.concatenate(
+        [masked(latents, layer_id, member, 0), masked(raw_partner, layer_id, 1 - member, 0)], 0
+    )
+    (own_all,) = tied(own_all)
+
+    goal_place = 2 * (feat_pos // 2 != member) + feat_pos % 2
+    chunk_cols = width_cols // CHUNKS
+    col_slices = [slice(c * chunk_cols, (c + 1) * chunk_cols) for c in range(CHUNKS)]
+    own_parts = []
+    for cols in col_slices:
+        goal = targets[:, cols].astype(jnp.float32)
+        none = jnp.zeros_like(goal)
+        goal = jnp.concatenate([jnp.where(goal_place == p, goal, none) for p in range(4)], 0)
+        own_parts.append(
+            jnp.dot(own_all, decoders[0, :, cols], preferred_element_type=jnp.float32) - goal
+        )
+
+    raw_pieces = []
+    for half, after in enumerate((CHUNKS - 2, CHUNKS)):
+        values = tied(raw_before[half], *own_parts[:after])
+        raw_pieces.append(values[0])
+        own_parts[:after] = values[1:]
+    prior_layer = jnp.maximum(layer_id - 1, 0)
+    prior_all = jnp.concatenate(
+        [
+            masked(rows, prior_layer, owner, half * half_rows)
+            for owner, held in (
+                (member, raw_pieces),
+                (1 - member, [swapped(piece, "layer", 0) for piece in raw_pieces]),
+            )
+            for half, rows in enumerate(held)
+        ],
+        0,
+    )
+    (prior_all,) = tied(prior_all)
+
+    def narrow(value):
+        return value.astype(jnp.bfloat16)
+
+    early, late = range(CHUNKS // 2), range(CHUNKS // 2, CHUNKS)
+    part_feats = feat_cols // PARTS
+    feat_slices = [slice(p * part_feats, (p + 1) * part_feats) for p in range(PARTS)]
+    jobs = [(span, p) for span in (1, 0) for p in range(PARTS)]
+
+    def term(rows, span, part, chunks):
+        cols = slice(chunks[0] * chunk_cols, (chunks[-1] + 1) * chunk_cols)
+        return lax.dot_general(
+            rows,
+            decoders[span, feat_slices[part], cols],
+            (((1,), (1,)), ((), ())),
+            preferred_element_type=jnp.float32,
+        )
+
+    def recon(rows, chunk):
+        return own_parts[chunk] + jnp.dot(
+            rows, decoders[1, :, col_slices[chunk]], preferred_element_type=jnp.float32
+        )
+
+    inner = (feat_pos == 1) | (feat_pos == 2)
+    routes = {"in": [(0, 1), (3, 2)], "across": [(1, 2), (2, 1)], "out": [(1, 0), (2, 3)]}
+    partial, total, errors = [None] * CHUNKS, [None] * CHUNKS, [None] * CHUNKS
+    partial[0] = recon(prior_all, 0)
+    first_wave = len(early) + 2
+    per_wave = len(jobs) // (CHUNKS + 2 - first_wave)
+    early_errors, early_terms = None, {}
+    for wave in range(CHUNKS + 2):
+        sent = {"rows": prior_all}
+        if wave < CHUNKS:
+            sent["in"] = narrow(partial[wave])
+        if 0 <= wave - 1 < CHUNKS:
+            sent["across"] = narrow(partial[wave - 1])
+        if 0 <= wave - 2 < CHUNKS:
+            sent["out"] = total[wave - 2]
+        if wave == first_wave:
+            early_errors = jnp.concatenate([errors[c] for c in early], 1)
+        if early_errors is not None:
+            sent["early"] = early_errors
+        held = dict(zip(sent, tied(*sent.values())))
+        got = {name: lax.ppermute(held[name], "feat", routes[name]) for name in routes if name in held}
+        if wave + 1 < CHUNKS:
+            got["next"] = recon(held["rows"], wave + 1)
+        if early_errors is not None:
+            early_errors = held["early"]
+            first_job = (wave - first_wave) * per_wave
+            for job in jobs[first_job : first_job + per_wave]:
+                got[job] = term(early_errors, *job, early)
+        got = dict(zip(got, tied(*got.values())))
+        if "next" in got:
+            partial[wave + 1] = got["next"]
+        if "in" in got:
+            partial[wave] = partial[wave] + got["in"].astype(jnp.float32)
+        if "across" in got:
+            total[wave - 1] = narrow(partial[wave - 1] + got["across"].astype(jnp.float32))
+        if "out" in got:
+            errors[wave - 2] = jnp.where(inner, held["out"], got["out"])
+        early_terms.update({job: got[job] for job in jobs if job in got})
+
+    late_errors = jnp.concatenate([errors[c] for c in late], 1)
+    held_terms, given, sums = [], [], []
+
+    def finish(step):
+        value = held_terms[step] + swapped(given[step], "layer", 0).astype(jnp.float32)
+        sums.append(narrow(value) if jobs[step][0] == 1 else value)
+
+    for step, job in enumerate(jobs):
+        if step >= 2:
+            finish(step - 2)
+            late_errors, sums[-1], given[-1] = tied(late_errors, sums[-1], given[-1])
+        elif step == 1:
+            late_errors, given[-1] = tied(late_errors, given[-1])
+        whole = early_terms[job] + term(late_errors, *job, late)
+        held_terms.append(whole[:held_rows])
+        given.append(narrow(whole[held_rows:]))
+    finish(len(jobs) - 2)
+    finish(len(jobs) - 1)
+    later = [passed_along(value, "layer", -2) for value in sums[:PARTS]]
+    pieces = [mine + more.astype(jnp.float32) for mine, more in zip(sums[PARTS:], later)]
+    latent_grad = masked(jnp.concatenate(pieces, 1), layer_id, member, 0)
+
+    error_rows = [jnp.concatenate(errors, 1)[p * half_rows : (p + 1) * half_rows] for p in range(4)]
+    errors_here = error_rows[3]
+    for p in range(3):
+        errors_here = jnp.where(goal_place == p, error_rows[p], errors_here)
+    return (errors_here, latent_grad)
+
+
 def solution(mesh):
     placed = (P("layer", "feat"), P(), P(None, "feat", "layer"), P("feat", "layer"))
+    on_line = mesh.shape["feat"] == 4 and mesh.shape["layer"] == 8
     return jax.shard_map(
-        local,
+        chain_local if on_line else local,
         mesh=mesh,
         in_specs=placed,
         out_specs=(P("feat", "layer"), P("layer", "feat")),

time: 515 us -> 324 us (0.63)
  waiting for transfers between devices: 377 us -> 68.3 us
  matrix products: 87 us -> 150 us
  starting transfers between devices: 7.17 us -> 60.3 us
  between operations: 14.2 us -> 2.16 us
  local copies, waits for them, and re-layouts: 3.05 us -> 14 us
    reduce_scatter x1 -> x0, waiting for transfers between devices: 147 us -> none  [local(): lax.psum_scatter(summed + jnp.dot(prior_all, decoders[1], preferred_eleme...]
    ppermute x2 -> x6, waiting for transfers between devices: 138 us -> 15.6 us  [passed_along(): lax.ppermute(value, axis, [(source, source + steps) for source in range(f...]
    all_gather x1 -> x0, waiting for transfers between devices: 81.6 us -> none  [local(): lax.all_gather(errors_here, 'feat', axis=0, tiled=True)]
    dot_general x3 -> x32, matrix products: 87 us -> 150 us  [the longest x16 72.9 us: term(): lax.dot_general(rows, decoders[span, feat_slices[part], cols], (((1,), (1...]
    ppermute x0 -> x24, waiting for transfers between devices: none -> 52 us  [chain_local(): lax.ppermute(held[name], 'feat', routes[name])]
    ppermute x0 -> x24, starting transfers between devices: none -> 42.5 us  [chain_local(): lax.ppermute(held[name], 'feat', routes[name])]
    ppermute x2 -> x11, waiting for transfers between devices: 11.1 us -> 0.77 us  [swapped(): return lax.ppermute(value, axis, pairs)]
    ppermute x2 -> x6, starting transfers between devices: 6.33 us -> 14.4 us  [passed_along(): lax.ppermute(value, axis, [(source, source + steps) for source in range(f...]
  transfers between devices with their start and end apart: 6 -> 41, of which waited for: 6 -> 16; matrix products, arithmetic and copies ran while one was open for 0% -> 44% of each run, Pallas kernels for 0% -> 0%
where the time goes in v1:
time: 324 us; the launch traced here: 319 us
  matrix products  150 us (46%)
  waiting for transfers between devices  68.3 us (21%)
  starting transfers between devices  60.3 us (19%)
  other arithmetic  24.1 us (7%)
  local copies, waits for them, and re-layouts  14 us (4%)
    dot_general x16, matrix products, term(): lax.dot_general(rows, decoders[span, feat_slices[part], cols], (((1,), (1...  72.9 us
    ppermute x24, waiting for transfers between devices, chain_local(): lax.ppermute(held[name], 'feat', routes[name])  52 us
    ppermute x24, starting transfers between devices, chain_local(): lax.ppermute(held[name], 'feat', routes[name])  42.5 us
    dot_general x8, matrix products, chain_local(): jnp.dot(own_all, decoders[0, :, cols], preferred_element_type=jnp.float32)  41.1 us
    dot_general x8, matrix products, recon(): jnp.dot(rows, decoders[1, :, col_slices[chunk]], preferred_element_type=j...  36.5 us
    ppermute x6, waiting for transfers between devices, passed_along(): lax.ppermute(value, axis, [(source, source + steps) for source in range(f...  15.6 us
    ppermute x6, starting transfers between devices, passed_along(): lax.ppermute(value, axis, [(source, source + steps) for source in range(f...  14.4 us
    broadcast_in_dim x12, local copies, waits for them, and re-layouts, masked(): tile_mask = jnp.repeat(jnp.repeat(hit, block_rows, axis=0), BLOCK, axis=1)  9.18 us
  transfers between devices with their start and end apart: 41, of which 16 were waited for; matrix products, arithmetic and copies ran while one was open for 44% of the time, Pallas kernels for 0%

profile of v1, /device:TPU:0, one launch (start us, length us, event | category | flops | bytes accessed | tf_op | source)
XLA Modules:
  0.0 319.3 jit_solution(9522985193991296128)
XLA Ops:
  4.3 5.5 %collective-permute-start = (bf16[128,4096]{1,0:T(8,128)(2,1)}, bf16[128,4096]{1,0:T(8,128)(2,1)}, u32[]{:S(2)}, u32[]{:S(2)}) collective-permute-start(bf16[128,4096]{1,0:T(8,128)(2,1)} %get-tuple-element.242), channel_id=1, source_target_pairs={{0,8},{4,12},{8,16},{12,20},{16,24},{20,28},{1,9},{5,13},{9,17},{1... | collective-permute-start | bytes 3145736 | tf_op jit(solution)/shard_map/ppermute | solution.py:21
  31.3 5.5 %fusion.108 = f32[512,512]{1,0:T(8,128)} fusion(bf16[512,4096]{1,0:T(8,128)(2,1)S(1)} %pad_maximum_fusion, bf16[2,4096,4096]{2,1,0:T(8,128)(2,1)} %param.6, f32[128,512]{1,0:T(8,128)S(1)} %get-tuple-element.257, f32[128,512]{1,0:T(8,128)S(1)} %get-tuple-element.258, f32[128,512]{1,0:T(8,128)S(1)} %get-tuple-element.273, f32[128,512]{1,0:T(8,128)S(1)} %get-tuple-element.267), kind=kOutput, calls=%fused_computation.111 | convolution fusion | flops 2148532224 | bytes 10485760 | tf_op jit(solution)/shard_map/dot_general | solution.py:140
  36.8 5.5 %fusion.105 = f32[512,512]{1,0:T(8,128)} fusion(bf16[512,4096]{1,0:T(8,128)(2,1)S(1)} %pad_maximum_fusion, bf16[2,4096,4096]{2,1,0:T(8,128)(2,1)} %param.6, f32[128,512]{1,0:T(8,128)S(1)} %get-tuple-element.254, f32[128,512]{1,0:T(8,128)S(1)} %get-tuple-element.255, f32[128,512]{1,0:T(8,128)S(1)} %get-tuple-element.256, f32[128,512]{1,0:T(8,128)S(1)} %get-tuple-element.268), kind=kOutput, calls=%fused_computation.110 | convolution fusion | flops 2148532224 | bytes 10485760 | tf_op jit(solution)/shard_map/dot_general | solution.py:140
  42.3 5.5 %fusion.102 = f32[512,512]{1,0:T(8,128)} fusion(bf16[512,4096]{1,0:T(8,128)(2,1)S(1)} %pad_maximum_fusion, bf16[2,4096,4096]{2,1,0:T(8,128)(2,1)} %param.6, f32[128,512]{1,0:T(8,128)S(1)} %get-tuple-element.251, f32[128,512]{1,0:T(8,128)S(1)} %get-tuple-element.252, f32[128,512]{1,0:T(8,128)S(1)} %get-tuple-element.253, f32[128,512]{1,0:T(8,128)S(1)} %get-tuple-element.269), kind=kOutput, calls=%fused_computation.109 | convolution fusion | flops 2148532224 | bytes 10485760 | tf_op jit(solution)/shard_map/dot_general | solution.py:140
  47.8 5.6 %fusion.99 = f32[512,512]{1,0:T(8,128)} fusion(bf16[512,4096]{1,0:T(8,128)(2,1)S(1)} %pad_maximum_fusion, bf16[2,4096,4096]{2,1,0:T(8,128)(2,1)} %param.6, f32[128,512]{1,0:T(8,128)S(1)} %get-tuple-element.248, f32[128,512]{1,0:T(8,128)S(1)} %get-tuple-element.249, f32[128,512]{1,0:T(8,128)S(1)} %get-tuple-element.250, f32[128,512]{1,0:T(8,128)S(1)} %get-tuple-element.270), kind=kOutput, calls=%fused_computation.108 | convolution fusion | flops 2148532224 | bytes 10485760 | tf_op jit(solution)/shard_map/dot_general | solution.py:140
  53.3 5.5 %fusion.96 = f32[512,512]{1,0:T(8,128)} fusion(bf16[512,4096]{1,0:T(8,128)(2,1)S(1)} %pad_maximum_fusion, bf16[2,4096,4096]{2,1,0:T(8,128)(2,1)} %param.6, f32[128,512]{1,0:T(8,128)S(1)} %get-tuple-element.245, f32[128,512]{1,0:T(8,128)S(1)} %get-tuple-element.246, f32[128,512]{1,0:T(8,128)S(1)} %get-tuple-element.247, f32[128,512]{1,0:T(8,128)S(1)} %get-tuple-element.271), kind=kOutput, calls=%fused_computation.107 | convolution fusion | flops 2148532224 | bytes 10485760 | tf_op jit(solution)/shard_map/dot_general | solution.py:140
  73.3 4.6 %fusion.46 = f32[512,512]{1,0:T(8,128)S(1)} fusion(bf16[512,4096]{1,0:T(8,128)(2,1)S(1)} %pad_maximum_fusion.1, bf16[2,4096,4096]{2,1,0:T(8,128)(2,1)} %param.6), kind=kOutput, calls=%fused_computation.49 | convolution fusion | flops 2147483648 | bytes 9437184 | tf_op jit(solution)/shard_map/dot_general | solution.py:180
  86.7 6.6 %collective-permute-done.5 = bf16[512,512]{1,0:T(8,128)(2,1)S(1)} collective-permute-done((bf16[512,512]{1,0:T(8,128)(2,1)S(1)}, bf16[512,512]{1,0:T(8,128)(2,1)S(1)}, u32[]{:S(2)}, u32[]{:S(2)}) %collective-permute-start.5) | collective-permute-done | bytes 524320 | tf_op jit(solution)/shard_map/ppermute | solution.py:204
  103.5 5.0 %collective-permute-done.6 = bf16[512,512]{1,0:T(8,128)(2,1)S(1)} collective-permute-done((bf16[512,512]{1,0:T(8,128)(2,1)S(1)}, bf16[512,512]{1,0:T(8,128)(2,1)S(1)}, u32[]{:S(2)}, u32[]{:S(2)}) %collective-permute-start.6) | collective-permute-done | bytes 524320 | tf_op jit(solution)/shard_map/ppermute | solution.py:204
  110.5 5.7 %collective-permute-start.8 = (bf16[512,512]{1,0:T(8,128)(2,1)S(1)}, bf16[512,512]{1,0:T(8,128)(2,1)S(1)}, u32[]{:S(2)}, u32[]{:S(2)}) collective-permute-start(bf16[512,512]{1,0:T(8,128)(2,1)S(1)} %convert_element_type.213), channel_id=1, source_target_pairs={{0,1},{3,2},{4,5},{7,6},{8,9},{11,10},{12,13},{15,14},{16,17},{19,... | collective-permute-start | bytes 1572872 | tf_op jit(solution)/shard_map/ppermute | solution.py:204
  126.4 5.8 %collective-permute-start.11 = (bf16[512,512]{1,0:T(8,128)(2,1)S(1)}, bf16[512,512]{1,0:T(8,128)(2,1)S(1)}, u32[]{:S(2)}, u32[]{:S(2)}) collective-permute-start(bf16[512,512]{1,0:T(8,128)(2,1)S(1)} %convert_element_type.218), channel_id=1, source_target_pairs={{0,1},{3,2},{4,5},{7,6},{8,9},{11,10},{12,13},{15,14},{16,17},{19,... | collective-permute-start | bytes 1572872 | tf_op jit(solution)/shard_map/ppermute | solution.py:204
  140.9 4.8 %collective-permute-done.13 = bf16[512,512]{1,0:T(8,128)(2,1)S(1)} collective-permute-done((bf16[512,512]{1,0:T(8,128)(2,1)S(1)}, bf16[512,512]{1,0:T(8,128)(2,1)S(1)}, u32[]{:S(2)}, u32[]{:S(2)}) %collective-permute-start.13) | collective-permute-done | bytes 524320 | tf_op jit(solution)/shard_map/ppermute | solution.py:204
  155.3 4.8 %collective-permute-done.16 = bf16[512,512]{1,0:T(8,128)(2,1)S(1)} collective-permute-done((bf16[512,512]{1,0:T(8,128)(2,1)S(1)}, bf16[512,512]{1,0:T(8,128)(2,1)S(1)}, u32[]{:S(2)}, u32[]{:S(2)}) %collective-permute-start.16) | collective-permute-done | bytes 524320 | tf_op jit(solution)/shard_map/ppermute | solution.py:204
  169.1 4.8 %collective-permute-done.19 = bf16[512,512]{1,0:T(8,128)(2,1)S(1)} collective-permute-done((bf16[512,512]{1,0:T(8,128)(2,1)S(1)}, bf16[512,512]{1,0:T(8,128)(2,1)S(1)}, u32[]{:S(2)}, u32[]{:S(2)}) %collective-permute-start.19) | collective-permute-done | bytes 524320 | tf_op jit(solution)/shard_map/ppermute | solution.py:204
  174.9 4.6 %fusion.32 = f32[512,512]{1,0:T(8,128)S(1)} fusion(bf16[512,4096]{1,0:T(8,128)(2,1)S(1)} %pad_maximum_fusion.1, bf16[2,4096,4096]{2,1,0:T(8,128)(2,1)} %param.6), kind=kOutput, calls=%fused_computation.35 | convolution fusion | flops 2147483648 | bytes 9437184 | tf_op jit(solution)/shard_map/dot_general | solution.py:180
  192.5 4.8 %collective-permute-done.22 = bf16[512,512]{1,0:T(8,128)(2,1)S(1)} collective-permute-done((bf16[512,512]{1,0:T(8,128)(2,1)S(1)}, bf16[512,512]{1,0:T(8,128)(2,1)S(1)}, u32[]{:S(2)}, u32[]{:S(2)}) %collective-permute-start.22) | collective-permute-done | bytes 524320 | tf_op jit(solution)/shard_map/ppermute | solution.py:204
  197.8 4.6 %fusion.24 = f32[512,1024]{1,0:T(8,128)S(1)} fusion(bf16[512,2048]{1,0:T(8,128)(2,1)S(1)} %pad_maximum_fusion.2, bf16[2,4096,4096]{2,1,0:T(8,128)(2,1)} %param.6), kind=kOutput, calls=%fused_computation.27 | convolution fusion | flops 2147483648 | bytes 8388608 | tf_op jit(solution)/shard_map/dot_general | solution.py:172
  210.6 5.0 %collective-permute-done.25 = bf16[512,512]{1,0:T(8,128)(2,1)S(1)} collective-permute-done((bf16[512,512]{1,0:T(8,128)(2,1)S(1)}, bf16[512,512]{1,0:T(8,128)(2,1)S(1)}, u32[]{:S(2)}, u32[]{:S(2)}) %collective-permute-start.25) | collective-permute-done | bytes 524320 | tf_op jit(solution)/shard_map/ppermute | solution.py:204
  227.4 5.3 %collective-permute-done.27 = bf16[512,512]{1,0:T(8,128)(2,1)S(1)} collective-permute-done((bf16[512,512]{1,0:T(8,128)(2,1)S(1)}, bf16[512,512]{1,0:T(8,128)(2,1)S(1)}, u32[]{:S(2)}, u32[]{:S(2)}) %collective-permute-start.27) | collective-permute-done | bytes 524320 | tf_op jit(solution)/shard_map/ppermute | solution.py:204
  244.0 4.6 %collective-permute-done.28 = bf16[512,512]{1,0:T(8,128)(2,1)S(1)} collective-permute-done((bf16[512,512]{1,0:T(8,128)(2,1)S(1)}, bf16[512,512]{1,0:T(8,128)(2,1)S(1)}, u32[]{:S(2)}, u32[]{:S(2)}) %collective-permute-start.28) | collective-permute-done | bytes 524320 | tf_op jit(solution)/shard_map/ppermute | solution.py:204
  248.8 4.7 %fusion.14 = f32[512,1024]{1,0:T(8,128)S(1)} fusion(bf16[2,4096,4096]{2,1,0:T(8,128)(2,1)} %param.6, bf16[512,512]{1,0:T(8,128)(2,1)S(1)} %get-tuple-element.225, bf16[512,512]{1,0:T(8,128)(2,1)S(1)} %get-tuple-element.227, bf16[512,512]{1,0:T(8,128)(2,1)S(1)} %get-tuple-element.229, bf16[512,512]{1,0:T(8,128)(2,1)S(1)} %get-tuple-element.231), kind=kOutput, calls=%fused_computation.17 | convolution fusion | flops 2155872256 | bytes 8388608 | tf_op jit(solution)/shard_map/dot_general | solution.py:172
  254.2 4.6 %fusion.12 = f32[512,1024]{1,0:T(8,128)S(1)} fusion(bf16[512,2048]{1,0:T(8,128)(2,1)S(1)} %pad_maximum_fusion.3, bf16[2,4096,4096]{2,1,0:T(8,128)(2,1)} %param.6), kind=kOutput, calls=%fused_computation.15 | convolution fusion | flops 2147483648 | bytes 8388608 | tf_op jit(solution)/shard_map/dot_general | solution.py:172
  300.6 5.2 %collective-permute-done.38 = bf16[256,1024]{1,0:T(8,128)(2,1)S(1)} collective-permute-done((bf16[256,1024]{1,0:T(8,128)(2,1)S(1)}, bf16[256,1024]{1,0:T(8,128)(2,1)S(1)}, u32[]{:S(2)}, u32[]{:S(2)}) %collective-permute-start.38) | collective-permute-done | bytes 524320 | tf_op jit(solution)/shard_map/ppermute | solution.py:21
  306.0 10.4 %collective-permute-done.40 = bf16[256,1024]{1,0:T(8,128)(2,1)S(1)} collective-permute-done((bf16[256,1024]{1,0:T(8,128)(2,1)S(1)}, bf16[256,1024]{1,0:T(8,128)(2,1)S(1)}, u32[]{:S(2)}, u32[]{:S(2)}) %collective-permute-start.40) | collective-permute-done | bytes 524320 | tf_op jit(solution)/shard_map/ppermute | solution.py:21
  (207 shorter events, 188.3 us)
Async XLA Ops:
  0.6 18.1 %collective-permute-start.1 = (bf16[256,4096]{1,0:T(8,128)(2,1)}, bf16[256,4096]{1,0:T(8,128)(2,1)S(1)}, u32[]{:S(2)}, u32[]{:S(2)}) collective-permute-start(bf16[256,4096]{1,0:T(8,128)(2,1)} %param.4), channel_id=1, source_target_pairs={{0,4},{4,0},{8,12},{12,8},{16,20},{20,16},{24,28},{28,24},{1,5},{5... | collective-permute-start | bytes 6291464 | tf_op jit(solution)/shard_map/ppermute | solution.py:15
  4.3 54.5 %collective-permute-start = (bf16[128,4096]{1,0:T(8,128)(2,1)}, bf16[128,4096]{1,0:T(8,128)(2,1)}, u32[]{:S(2)}, u32[]{:S(2)}) collective-permute-start(bf16[128,4096]{1,0:T(8,128)(2,1)} %get-tuple-element.242), channel_id=1, source_target_pairs={{0,8},{4,12},{8,16},{12,20},{16,24},{20,28},{1,9},{5,13},{9,17},{1... | collective-permute-start | bytes 3145736 | tf_op jit(solution)/shard_map/ppermute | solution.py:21
  9.7 53.6 %collective-permute-start.2 = (bf16[128,4096]{1,0:T(8,128)(2,1)}, bf16[128,4096]{1,0:T(8,128)(2,1)}, u32[]{:S(2)}, u32[]{:S(2)}) collective-permute-start(bf16[128,4096]{1,0:T(8,128)(2,1)} %get-tuple-element.243), channel_id=1, source_target_pairs={{0,8},{4,12},{8,16},{12,20},{16,24},{20,28},{1,9},{5,13},{9,17},{1... | collective-permute-start | bytes 3145736 | tf_op jit(solution)/shard_map/ppermute | solution.py:21
  78.2 15.0 %collective-permute-start.5 = (bf16[512,512]{1,0:T(8,128)(2,1)S(1)}, bf16[512,512]{1,0:T(8,128)(2,1)S(1)}, u32[]{:S(2)}, u32[]{:S(2)}) collective-permute-start(bf16[512,512]{1,0:T(8,128)(2,1)S(1)} %get-tuple-element.121), channel_id=1, source_target_pairs={{0,1},{3,2},{4,5},{7,6},{8,9},{11,10},{12,13},{15,14},{16,17},{19,... | collective-permute-start | bytes 1572872 | tf_op jit(solution)/shard_map/ppermute | solution.py:204
  93.5 15.0 %collective-permute-start.6 = (bf16[512,512]{1,0:T(8,128)(2,1)S(1)}, bf16[512,512]{1,0:T(8,128)(2,1)S(1)}, u32[]{:S(2)}, u32[]{:S(2)}) collective-permute-start(bf16[512,512]{1,0:T(8,128)(2,1)S(1)} %convert_element_type.210), channel_id=1, source_target_pairs={{0,1},{3,2},{4,5},{7,6},{8,9},{11,10},{12,13},{15,14},{16,17},{19,... | collective-permute-start | bytes 1572872 | tf_op jit(solution)/shard_map/ppermute | solution.py:204
  98.0 10.5 %collective-permute-start.7 = (bf16[512,512]{1,0:T(8,128)(2,1)S(1)}, bf16[512,512]{1,0:T(8,128)(2,1)S(1)}, u32[]{:S(2)}, u32[]{:S(2)}) collective-permute-start(bf16[512,512]{1,0:T(8,128)(2,1)S(1)} %fusion.128), channel_id=1, source_target_pairs={{1,2},{2,1},{5,6},{6,5},{9,10},{10,9},{13,14},{14,13},{17,18},{18,... | collective-permute-start | bytes 1572872 | tf_op jit(solution)/shard_map/ppermute | solution.py:204
  109.0 15.5 %collective-permute-start.10 = (bf16[512,512]{1,0:T(8,128)(2,1)S(1)}, bf16[512,512]{1,0:T(8,128)(2,1)S(1)}, u32[]{:S(2)}, u32[]{:S(2)}) collective-permute-start(bf16[512,512]{1,0:T(8,128)(2,1)S(1)} %add_convert_fusion.7), channel_id=1, source_target_pairs={{1,0},{2,3},{5,4},{6,7},{9,8},{10,11},{13,12},{14,15},{17,16},{18,... | collective-permute-start | bytes 1572872 | tf_op jit(solution)/shard_map/ppermute | solution.py:204
  110.5 15.3 %collective-permute-start.8 = (bf16[512,512]{1,0:T(8,128)(2,1)S(1)}, bf16[512,512]{1,0:T(8,128)(2,1)S(1)}, u32[]{:S(2)}, u32[]{:S(2)}) collective-permute-start(bf16[512,512]{1,0:T(8,128)(2,1)S(1)} %convert_element_type.213), channel_id=1, source_target_pairs={{0,1},{3,2},{4,5},{7,6},{8,9},{11,10},{12,13},{15,14},{16,17},{19,... | collective-permute-start | bytes 1572872 | tf_op jit(solution)/shard_map/ppermute | solution.py:204
  116.2 9.6 %collective-permute-start.9 = (bf16[512,512]{1,0:T(8,128)(2,1)S(1)}, bf16[512,512]{1,0:T(8,128)(2,1)S(1)}, u32[]{:S(2)}, u32[]{:S(2)}) collective-permute-start(bf16[512,512]{1,0:T(8,128)(2,1)S(1)} %fusion.129), channel_id=1, source_target_pairs={{1,2},{2,1},{5,6},{6,5},{9,10},{10,9},{13,14},{14,13},{17,18},{18,... | collective-permute-start | bytes 1572872 | tf_op jit(solution)/shard_map/ppermute | solution.py:204
  126.4 14.5 %collective-permute-start.11 = (bf16[512,512]{1,0:T(8,128)(2,1)S(1)}, bf16[512,512]{1,0:T(8,128)(2,1)S(1)}, u32[]{:S(2)}, u32[]{:S(2)}) collective-permute-start(bf16[512,512]{1,0:T(8,128)(2,1)S(1)} %convert_element_type.218), channel_id=1, source_target_pairs={{0,1},{3,2},{4,5},{7,6},{8,9},{11,10},{12,13},{15,14},{16,17},{19,... | collective-permute-start | bytes 1572872 | tf_op jit(solution)/shard_map/ppermute | solution.py:204
  132.9 12.8 %collective-permute-start.13 = (bf16[512,512]{1,0:T(8,128)(2,1)S(1)}, bf16[512,512]{1,0:T(8,128)(2,1)S(1)}, u32[]{:S(2)}, u32[]{:S(2)}) collective-permute-start(bf16[512,512]{1,0:T(8,128)(2,1)S(1)} %add_convert_fusion.6), channel_id=1, source_target_pairs={{1,0},{2,3},{5,4},{6,7},{9,8},{10,11},{13,12},{14,15},{17,16},{18,... | collective-permute-start | bytes 1572872 | tf_op jit(solution)/shard_map/ppermute | solution.py:204
  146.2 9.1 %collective-permute-start.14 = (bf16[512,512]{1,0:T(8,128)(2,1)S(1)}, bf16[512,512]{1,0:T(8,128)(2,1)S(1)}, u32[]{:S(2)}, u32[]{:S(2)}) collective-permute-start(bf16[512,512]{1,0:T(8,128)(2,1)S(1)} %convert_element_type.223), channel_id=1, source_target_pairs={{0,1},{3,2},{4,5},{7,6},{8,9},{11,10},{12,13},{15,14},{16,17},{19,... | collective-permute-start | bytes 1572872 | tf_op jit(solution)/shard_map/ppermute | solution.py:204
  148.4 11.7 %collective-permute-start.16 = (bf16[512,512]{1,0:T(8,128)(2,1)S(1)}, bf16[512,512]{1,0:T(8,128)(2,1)S(1)}, u32[]{:S(2)}, u32[]{:S(2)}) collective-permute-start(bf16[512,512]{1,0:T(8,128)(2,1)S(1)} %add_convert_fusion.5), channel_id=1, source_target_pairs={{1,0},{2,3},{5,4},{6,7},{9,8},{10,11},{13,12},{14,15},{17,16},{18,... | collective-permute-start | bytes 1572872 | tf_op jit(solution)/shard_map/ppermute | solution.py:204
  162.9 11.1 %collective-permute-start.19 = (bf16[512,512]{1,0:T(8,128)(2,1)S(1)}, bf16[512,512]{1,0:T(8,128)(2,1)S(1)}, u32[]{:S(2)}, u32[]{:S(2)}) collective-permute-start(bf16[512,512]{1,0:T(8,128)(2,1)S(1)} %add_convert_fusion.4), channel_id=1, source_target_pairs={{1,0},{2,3},{5,4},{6,7},{9,8},{10,11},{13,12},{14,15},{17,16},{18,... | collective-permute-start | bytes 1572872 | tf_op jit(solution)/shard_map/ppermute | solution.py:204
  186.2 11.1 %collective-permute-start.22 = (bf16[512,512]{1,0:T(8,128)(2,1)S(1)}, bf16[512,512]{1,0:T(8,128)(2,1)S(1)}, u32[]{:S(2)}, u32[]{:S(2)}) collective-permute-start(bf16[512,512]{1,0:T(8,128)(2,1)S(1)} %add_convert_fusion.3), channel_id=1, source_target_pairs={{1,0},{2,3},{5,4},{6,7},{9,8},{10,11},{13,12},{14,15},{17,16},{18,... | collective-permute-start | bytes 1572872 | tf_op jit(solution)/shard_map/ppermute | solution.py:204
  204.6 11.1 %collective-permute-start.25 = (bf16[512,512]{1,0:T(8,128)(2,1)S(1)}, bf16[512,512]{1,0:T(8,128)(2,1)S(1)}, u32[]{:S(2)}, u32[]{:S(2)}) collective-permute-start(bf16[512,512]{1,0:T(8,128)(2,1)S(1)} %add_convert_fusion.2), channel_id=1, source_target_pairs={{1,0},{2,3},{5,4},{6,7},{9,8},{10,11},{13,12},{14,15},{17,16},{18,... | collective-permute-start | bytes 1572872 | tf_op jit(solution)/shard_map/ppermute | solution.py:204
  221.3 11.4 %collective-permute-start.27 = (bf16[512,512]{1,0:T(8,128)(2,1)S(1)}, bf16[512,512]{1,0:T(8,128)(2,1)S(1)}, u32[]{:S(2)}, u32[]{:S(2)}) collective-permute-start(bf16[512,512]{1,0:T(8,128)(2,1)S(1)} %add_convert_fusion.1), channel_id=1, source_target_pairs={{1,0},{2,3},{5,4},{6,7},{9,8},{10,11},{13,12},{14,15},{17,16},{18,... | collective-permute-start | bytes 1572872 | tf_op jit(solution)/shard_map/ppermute | solution.py:204
  237.5 11.1 %collective-permute-start.28 = (bf16[512,512]{1,0:T(8,128)(2,1)S(1)}, bf16[512,512]{1,0:T(8,128)(2,1)S(1)}, u32[]{:S(2)}, u32[]{:S(2)}) collective-permute-start(bf16[512,512]{1,0:T(8,128)(2,1)S(1)} %add_convert_fusion), channel_id=1, source_target_pairs={{1,0},{2,3},{5,4},{6,7},{9,8},{10,11},{13,12},{14,15},{17,16},{18,... | collective-permute-start | bytes 1572872 | tf_op jit(solution)/shard_map/ppermute | solution.py:204
  266.6 27.7 %collective-permute-start.34 = (bf16[256,1024]{1,0:T(8,128)(2,1)S(1)}, bf16[256,1024]{1,0:T(8,128)(2,1)S(1)}, u32[]{:S(2)}, u32[]{:S(2)}) collective-permute-start(bf16[256,1024]{1,0:T(8,128)(2,1)S(1)} %fusion.125), channel_id=1, source_target_pairs={{8,0},{12,4},{16,8},{20,12},{24,16},{28,20},{9,1},{13,5},{17,9},{2... | collective-permute-start | bytes 1572872 | tf_op jit(solution)/shard_map/ppermute | solution.py:21
  273.7 26.6 %collective-permute-start.36 = (bf16[256,1024]{1,0:T(8,128)(2,1)S(1)}, bf16[256,1024]{1,0:T(8,128)(2,1)S(1)}, u32[]{:S(2)}, u32[]{:S(2)}) collective-permute-start(bf16[256,1024]{1,0:T(8,128)(2,1)S(1)} %fusion.124), channel_id=1, source_target_pairs={{8,0},{12,4},{16,8},{20,12},{24,16},{28,20},{9,1},{13,5},{17,9},{2... | collective-permute-start | bytes 1572872 | tf_op jit(solution)/shard_map/ppermute | solution.py:21
  280.4 25.3 %collective-permute-start.38 = (bf16[256,1024]{1,0:T(8,128)(2,1)S(1)}, bf16[256,1024]{1,0:T(8,128)(2,1)S(1)}, u32[]{:S(2)}, u32[]{:S(2)}) collective-permute-start(bf16[256,1024]{1,0:T(8,128)(2,1)S(1)} %fusion.123), channel_id=1, source_target_pairs={{8,0},{12,4},{16,8},{20,12},{24,16},{28,20},{9,1},{13,5},{17,9},{2... | collective-permute-start | bytes 1572872 | tf_op jit(solution)/shard_map/ppermute | solution.py:21
  287.4 29.0 %collective-permute-start.40 = (bf16[256,1024]{1,0:T(8,128)(2,1)S(1)}, bf16[256,1024]{1,0:T(8,128)(2,1)S(1)}, u32[]{:S(2)}, u32[]{:S(2)}) collective-permute-start(bf16[256,1024]{1,0:T(8,128)(2,1)S(1)} %fusion.122), channel_id=1, source_target_pairs={{8,0},{12,4},{16,8},{20,12},{24,16},{28,20},{9,1},{13,5},{17,9},{2... | collective-permute-start | bytes 1572872 | tf_op jit(solution)/shard_map/ppermute | solution.py:21
  294.7 11.0 %collective-permute-start.37 = (bf16[256,1024]{1,0:T(8,128)(2,1)S(1)}, bf16[256,1024]{1,0:T(8,128)(2,1)S(1)}, u32[]{:S(2)}, u32[]{:S(2)}) collective-permute-start(bf16[256,1024]{1,0:T(8,128)(2,1)S(1)} %slice.489), channel_id=1, source_target_pairs={{0,4},{4,0},{8,12},{12,8},{16,20},{20,16},{24,28},{28,24},{1,5},{5... | collective-permute-start | bytes 1572872 | tf_op jit(solution)/shard_map/ppermute | solution.py:15
  300.2 16.2 %collective-permute-start.39 = (bf16[256,1024]{1,0:T(8,128)(2,1)S(1)}, bf16[256,1024]{1,0:T(8,128)(2,1)S(1)}, u32[]{:S(2)}, u32[]{:S(2)}) collective-permute-start(bf16[256,1024]{1,0:T(8,128)(2,1)S(1)} %slice.488), channel_id=1, source_target_pairs={{0,4},{4,0},{8,12},{12,8},{16,20},{20,16},{24,28},{28,24},{1,5},{5... | collective-permute-start | bytes 1572872 | tf_op jit(solution)/shard_map/ppermute | solution.py:15
  (27 other events, 211.4 us)

commit v2 on v0

--- a/solution.py
+++ b/solution.py
@@ -1,10 +1,16 @@
+import functools
+
 import jax
 import jax.numpy as jnp
 from jax import lax
+from jax.experimental import pallas as pl
+from jax.experimental.pallas import tpu as pltpu
 from jax.sharding import PartitionSpec as P
 
 D = 8192
 BLOCK = 128
+CHUNKS = 32
+PARTS = 4
 
 
 def swapped(value, axis, bit):
@@ -88,10 +94,217 @@
     return (errors_here, latent_grad)
 
 
+def line_kernel(
+    chunks, partial, errors, sent, got_in, got_across, in_out, in_in, over_out, over_in, back_out, back_in
+):
+    me = lax.axis_index("feat")
+    partner = me + 1 - 2 * (me % 2)
+    inner = (me == 1) | (me == 2)
+    rows = partial.shape[0] // chunks
+
+    def block(c):
+        return pl.ds(pl.multiple_of(c * rows, rows), rows)
+
+    def copy(c, source, target, out_sems, in_sems, owner):
+        return pltpu.make_async_remote_copy(
+            src_ref=source.at[block(c)],
+            dst_ref=target.at[block(c)],
+            send_sem=out_sems.at[c],
+            recv_sem=in_sems.at[c],
+            device_id={"feat": owner},
+            device_id_type=pl.DeviceIdType.MESH,
+        )
+
+    def inward(c):
+        return copy(c, sent, got_in, in_out, in_in, partner)
+
+    def across(c):
+        return copy(c, sent, got_across, over_out, over_in, 3 - me)
+
+    def outward(c):
+        return copy(c, errors, errors, back_out, back_in, partner)
+
+    def each(first, last, body):
+        def step(c, carry):
+            body(c)
+            return carry
+
+        lax.fori_loop(first, last, step, 0)
+
+    barrier = pltpu.get_barrier_semaphore()
+    pl.semaphore_signal(
+        barrier, inc=1, device_id={"feat": partner}, device_id_type=pl.DeviceIdType.MESH
+    )
+
+    @pl.when(inner)
+    def _():
+        pl.semaphore_signal(
+            barrier, inc=1, device_id={"feat": 3 - me}, device_id_type=pl.DeviceIdType.MESH
+        )
+        pl.semaphore_wait(barrier, 2)
+
+        def gather(c):
+            inward(c).wait_recv()
+            total = partial[block(c), :] + got_in[block(c), :].astype(jnp.float32)
+            sent[block(c), :] = total.astype(jnp.bfloat16)
+            across(c).start()
+
+        def spread(c):
+            across(c).wait_recv()
+            total = sent[block(c), :].astype(jnp.float32) + got_across[block(c), :].astype(jnp.float32)
+            errors[block(c), :] = total.astype(jnp.bfloat16)
+            outward(c).start()
+
+        def both(c):
+            gather(c)
+            spread(c - 1)
+
+        gather(0)
+        each(1, chunks, both)
+        spread(chunks - 1)
+
+        def drain(c):
+            across(c).wait_send()
+            outward(c).wait_send()
+
+        each(0, chunks, drain)
+
+    @pl.when(jnp.logical_not(inner))
+    def _():
+        pl.semaphore_wait(barrier, 1)
+
+        def send(c):
+            sent[block(c), :] = partial[block(c), :].astype(jnp.bfloat16)
+            inward(c).start()
+
+        def drain(c):
+            inward(c).wait_send()
+            outward(c).wait_recv()
+
+        each(0, chunks, send)
+        each(0, chunks, drain)
+
+
+def summed_on_line(partial):
+    shape = partial.shape
+    return pl.pallas_call(
+        functools.partial(line_kernel, CHUNKS),
+        out_shape=jax.ShapeDtypeStruct(shape, jnp.bfloat16),
+        in_specs=[pl.BlockSpec(memory_space=pltpu.VMEM)],
+        out_specs=pl.BlockSpec(memory_space=pltpu.VMEM),
+        scratch_shapes=[pltpu.VMEM(shape, jnp.bfloat16)] * 3
+        + [pltpu.SemaphoreType.DMA((CHUNKS,))] * 6,
+        compiler_params=pltpu.CompilerParams(
+            collective_id=0, has_side_effects=True, vmem_limit_bytes=48 * 1024 * 1024
+        ),
+        cost_estimate=pl.CostEstimate(
+            flops=4 * shape[0] * shape[1], bytes_accessed=6 * shape[0] * shape[1], transcendentals=0
+        ),
+    )(partial)
+
+
+def tied(*values):
+    return lax.optimization_barrier(values)
+
+
+def chain_local(latents, block_lists, decoders, targets):
+    layer_pos = lax.axis_index("layer")
+    feat_pos = lax.axis_index("feat")
+    width_cols = decoders.shape[2]
+    layer_id = layer_pos // 2
+    member = layer_pos % 2
+    held_rows, feat_cols = latents.shape
+    half_rows = held_rows // 2
+    tok_blocks = block_lists.shape[1]
+    block_rows = 2 * held_rows // tok_blocks
+    blocks_here = feat_cols // BLOCK
+
+    raw_before = passed_along(latents, "layer", 2)
+    raw_partner = swapped(latents, "layer", 0)
+    wanted = feat_pos * blocks_here + jnp.arange(blocks_here, dtype=jnp.int32)
+
+    def mask_of(layer, owner):
+        lists = lax.dynamic_index_in_dim(block_lists, layer, 0, keepdims=False)
+        hit = jnp.any(lists[:, :, None] == wanted[None, None, :], axis=1)
+        count = tok_blocks // 2
+        hit = lax.dynamic_slice_in_dim(hit, owner * count, count, 0)
+        return jnp.repeat(jnp.repeat(hit, block_rows, axis=0), BLOCK, axis=1)
+
+    def masked(rows, mask):
+        return jnp.where(mask, rows, jnp.zeros_like(rows))
+
+    prior_layer = jnp.maximum(layer_id - 1, 0)
+    own_mask = mask_of(layer_id, member)
+    own_all = jnp.concatenate(
+        [masked(latents, own_mask), masked(raw_partner, mask_of(layer_id, 1 - member))], 0
+    )
+    own_all, prior_mask, prior_mask_partner = tied(
+        own_all, mask_of(prior_layer, member), mask_of(prior_layer, 1 - member)
+    )
+
+    goal_place = 2 * (feat_pos // 2 != member) + feat_pos % 2
+    own_part = jnp.dot(own_all, decoders[0], preferred_element_type=jnp.float32)
+
+    raw_prior, own_part = tied(raw_before, own_part)
+    prior_all = jnp.concatenate(
+        [
+            masked(raw_prior, prior_mask),
+            masked(swapped(raw_prior, "layer", 0), prior_mask_partner),
+        ],
+        0,
+    )
+    (prior_all,) = tied(prior_all)
+
+    def narrow(value):
+        return value.astype(jnp.bfloat16)
+
+    goal = targets.astype(jnp.float32)
+    none = jnp.zeros_like(goal)
+    goal = jnp.concatenate([jnp.where(goal_place == p, goal, none) for p in range(4)], 0)
+    partial = own_part + jnp.dot(prior_all, decoders[1], preferred_element_type=jnp.float32)
+    errors = summed_on_line(partial - goal)
+
+    jobs = [(span, p) for span in (1, 0) for p in range(PARTS)]
+    held_terms, given, sums = [], [], []
+    size = feat_cols // PARTS
+
+    def finish(step):
+        value = held_terms[step] + swapped(given[step], "layer", 0).astype(jnp.float32)
+        sums.append(narrow(value) if jobs[step][0] == 1 else value)
+
+    rows = errors
+    for step, (span, part) in enumerate(jobs):
+        if step >= 2:
+            finish(step - 2)
+            rows, sums[-1], given[-1] = tied(rows, sums[-1], given[-1])
+        elif step == 1:
+            rows, given[-1] = tied(rows, given[-1])
+        term = lax.dot_general(
+            rows,
+            decoders[span, part * size : (part + 1) * size],
+            (((1,), (1,)), ((), ())),
+            preferred_element_type=jnp.float32,
+        )
+        held_terms.append(term[:held_rows])
+        given.append(narrow(term[held_rows:]))
+    finish(len(jobs) - 2)
+    finish(len(jobs) - 1)
+    later = [passed_along(value, "layer", -2) for value in sums[:PARTS]]
+    pieces = [mine + more.astype(jnp.float32) for mine, more in zip(sums[PARTS:], later)]
+    latent_grad = masked(jnp.concatenate(pieces, 1), own_mask)
+
+    error_rows = [errors[p * half_rows : (p + 1) * half_rows] for p in range(4)]
+    errors_here = error_rows[3]
+    for p in range(3):
+        errors_here = jnp.where(goal_place == p, error_rows[p], errors_here)
+    return (errors_here, latent_grad)
+
+
 def solution(mesh):
     placed = (P("layer", "feat"), P(), P(None, "feat", "layer"), P("feat", "layer"))
+    on_line = mesh.shape["feat"] == 4 and mesh.shape["layer"] == 8
     return jax.shard_map(
-        local,
+        chain_local if on_line else local,
         mesh=mesh,
         in_specs=placed,
         out_specs=(P("feat", "layer"), P("layer", "feat")),

time: 515 us -> 273 us (0.53)
  waiting for transfers between devices: 377 us -> 8.5 us
  Pallas kernels: 0 us -> 108 us
  matrix products: 87 us -> 102 us
  between operations: 14.2 us -> 1.13 us
  local copies, waits for them, and re-layouts: 3.05 us -> 12.1 us
  starting transfers between devices: 7.17 us -> 14.1 us
    reduce_scatter x1 -> x0, waiting for transfers between devices: 147 us -> none  [local(): lax.psum_scatter(summed + jnp.dot(prior_all, decoders[1], preferred_eleme...]
    ppermute x2 -> x5, waiting for transfers between devices: 138 us -> 5.89 us  [passed_along(): lax.ppermute(value, axis, [(source, source + steps) for source in range(f...]
    pallas_call x0 -> x1, Pallas kernels: none -> 108 us  [summed_on_line(): pl.pallas_call(functools.partial(line_kernel, CHUNKS), out_shape=jax.Shap...]
    all_gather x1 -> x0, waiting for transfers between devices: 81.6 us -> none  [local(): lax.all_gather(errors_here, 'feat', axis=0, tiled=True)]
    dot_general x3 -> x10, matrix products: 87 us -> 102 us  [the longest x8 56.1 us: chain_local(): lax.dot_general(rows, decoders[span, part * size:(part + 1) * size], (((1...]
    sub x0 -> x1, other arithmetic: none -> 9.22 us  [chain_local(): errors = summed_on_line(partial - goal)]
    ppermute x2 -> x10, waiting for transfers between devices: 11.1 us -> 2.61 us  [swapped(): return lax.ppermute(value, axis, pairs)]
    convert_element_type x2 -> x4, other arithmetic: 9.01 us -> 0.63 us  [narrow(): return value.astype(jnp.bfloat16)]
  transfers between devices with their start and end apart: 6 -> 15, of which waited for: 6 -> 3; matrix products, arithmetic and copies ran while one was open for 0% -> 34% of each run, Pallas kernels for 0% -> 0%
where the time goes in v2:
time: 273 us; the launch traced here: 268 us
  Pallas kernels  108 us (40%)
  matrix products  102 us (37%)
  other arithmetic  21.7 us (8%)
  starting transfers between devices  14.1 us (5%)
  local copies, waits for them, and re-layouts  12.1 us (4%)
  waiting for transfers between devices  8.5 us (3%)
    pallas_call x1, Pallas kernels, summed_on_line(): pl.pallas_call(functools.partial(line_kernel, CHUNKS), out_shape=jax.Shap...  108 us
    dot_general x8, matrix products, chain_local(): lax.dot_general(rows, decoders[span, part * size:(part + 1) * size], (((1...  56.1 us
    dot_general x1, matrix products, chain_local(): jnp.dot(prior_all, decoders[1], preferred_element_type=jnp.float32)  23.2 us
    dot_general x1, matrix products, chain_local(): own_part = jnp.dot(own_all, decoders[0], preferred_element_type=jnp.float32)  23.1 us
    ppermute x5, starting transfers between devices, passed_along(): lax.ppermute(value, axis, [(source, source + steps) for source in range(f...  11 us
    sub x1, other arithmetic, chain_local(): errors = summed_on_line(partial - goal)  9.22 us
    broadcast_in_dim x8, local copies, waits for them, and re-layouts, mask_of(): return jnp.repeat(jnp.repeat(hit, block_rows, axis=0), BLOCK, axis=1)  8.29 us
    select_n x5, other arithmetic, masked(): return jnp.where(mask, rows, jnp.zeros_like(rows))  7.24 us
  transfers between devices with their start and end apart: 15, of which 3 were waited for; matrix products, arithmetic and copies ran while one was open for 34% of the time, Pallas kernels for 0%

profile of v2, /device:TPU:0, one launch (start us, length us, event | category | flops | bytes accessed | tf_op | source)
XLA Modules:
  0.0 268.2 jit_solution(5709857496876724219)
XLA Ops:
  1.2 5.9 %collective-permute-start = (bf16[256,4096]{1,0:T(8,128)(2,1)}, bf16[256,4096]{1,0:T(8,128)(2,1)}, u32[]{:S(2)}, u32[]{:S(2)}) collective-permute-start(bf16[256,4096]{1,0:T(8,128)(2,1)} %param.4), channel_id=1, source_target_pairs={{0,8},{4,12},{8,16},{12,20},{16,24},{20,28},{1,9},{5,13},{9,17},{1... | collective-permute-start | bytes 6291464 | tf_op jit(solution)/shard_map/ppermute | solution.py:25
  8.6 2.1 broadcast_in_dim.43
  11.4 2.1 broadcast_in_dim.45
  14.3 2.1 broadcast_in_dim.39
  17.9 2.1 broadcast_in_dim.41
  20.0 2.2 bitcast_select_fusion
  22.5 23.1 %fusion.2 = f32[512,4096]{1,0:T(8,128)} fusion(bf16[512,4096]{1,0:T(8,128)(2,1)S(1)} %pad_maximum_fusion, bf16[2,4096,4096]{2,1,0:T(8,128)(2,1)} %param.6), kind=kOutput, calls=%fused_computation.2 | convolution fusion | flops 17179869184 | bytes 46137344 | tf_op jit(solution)/shard_map/dot_general | solution.py:246
  45.5 5.9 %collective-permute-done = bf16[256,4096]{1,0:T(8,128)(2,1)} collective-permute-done((bf16[256,4096]{1,0:T(8,128)(2,1)}, bf16[256,4096]{1,0:T(8,128)(2,1)}, u32[]{:S(2)}, u32[]{:S(2)}) %collective-permute-start) | collective-permute-done | bytes 2097184 | tf_op jit(solution)/shard_map/ppermute | solution.py:25
  52.4 1.9 broadcast_select_fusion.1
  54.3 1.5 collective-permute-done.2
  56.3 23.2 %fusion = f32[512,4096]{1,0:T(8,128)} fusion(bf16[512,4096]{1,0:T(8,128)(2,1)S(1)} %pad_maximum_fusion.1, bf16[2,4096,4096]{2,1,0:T(8,128)(2,1)} %param.6), kind=kOutput, calls=%fused_computation | convolution fusion | flops 17179869184 | bytes 46137344 | tf_op jit(solution)/shard_map/dot_general | solution.py:264
  79.4 9.2 %maximum_subtract_fusion.partial = f32[512,4096]{1,0:T(8,128)} fusion(f32[128,4096]{1,0:T(8,128)S(1)} %get-tuple-element.57, f32[128,4096]{1,0:T(8,128)S(1)} %get-tuple-element.56, f32[128,4096]{1,0:T(8,128)S(1)} %get-tuple-element.55, f32[128,4096]{1,0:T(8,128)S(1)} %get-tuple-element.54, f32[512,4096]{1,0:T(8,128)} %fusion.2, f32[512,4096]{1,0:T(8,128)} %fusion), kind=kLoop, calls=%fused_computation.6 | loop fusion | flops 10485760 | bytes 33554432 | tf_op jit(solution)/shard_map/sub | solution.py:265
  88.7 108.4 %shard_map.59 = bf16[512,4096]{1,0:T(8,128)(2,1)S(1)} custom-call(f32[512,4096]{1,0:T(8,128)} %maximum_subtract_fusion.partial), custom_call_target="tpu_custom_call" | custom-call | flops 8388608 | bytes 12582912 | tf_op jit(solution)/shard_map/pallas_call | solution.py:190
  197.1 7.0 %fusion.20 = f32[512,1024]{1,0:T(8,128)S(1)} fusion(bf16[512,4096]{1,0:T(8,128)(2,1)S(1)} %shard_map.59, bf16[2,4096,4096]{2,1,0:T(8,128)(2,1)} %param.6), kind=kOutput, calls=%fused_computation.21 | convolution fusion | flops 4294967296 | bytes 14680064 | tf_op jit(solution)/shard_map/dot_general | solution.py:282
  204.2 6.9 %fusion.18 = f32[512,1024]{1,0:T(8,128)S(1)} fusion(bf16[512,4096]{1,0:T(8,128)(2,1)S(1)} %shard_map.59, bf16[2,4096,4096]{2,1,0:T(8,128)(2,1)} %param.6), kind=kOutput, calls=%fused_computation.19 | convolution fusion | flops 4294967296 | bytes 14680064 | tf_op jit(solution)/shard_map/dot_general | solution.py:282
  213.1 1.3 collective-permute-start.8
  214.4 7.2 %fusion.16 = f32[512,1024]{1,0:T(8,128)S(1)} fusion(bf16[512,4096]{1,0:T(8,128)(2,1)S(1)} %shard_map.59, bf16[2,4096,4096]{2,1,0:T(8,128)(2,1)} %param.6), kind=kOutput, calls=%fused_computation.17 | convolution fusion | flops 4294967296 | bytes 14680064 | tf_op jit(solution)/shard_map/dot_general | solution.py:282
  222.0 1.3 collective-permute-start.10
  223.2 6.9 %fusion.14 = f32[512,1024]{1,0:T(8,128)S(1)} fusion(bf16[512,4096]{1,0:T(8,128)(2,1)S(1)} %shard_map.59, bf16[2,4096,4096]{2,1,0:T(8,128)(2,1)} %param.6), kind=kOutput, calls=%fused_computation.15 | convolution fusion | flops 4294967296 | bytes 14680064 | tf_op jit(solution)/shard_map/dot_general | solution.py:282
  232.3 6.9 %fusion.12 = f32[512,1024]{1,0:T(8,128)S(1)} fusion(bf16[512,4096]{1,0:T(8,128)(2,1)S(1)} %shard_map.59, bf16[2,4096,4096]{2,1,0:T(8,128)(2,1)} %param.6), kind=kOutput, calls=%fused_computation.13 | convolution fusion | flops 4294967296 | bytes 14680064 | tf_op jit(solution)/shard_map/dot_general | solution.py:282
  240.9 7.2 %fusion.10 = f32[512,1024]{1,0:T(8,128)S(1)} fusion(bf16[512,4096]{1,0:T(8,128)(2,1)S(1)} %shard_map.59, bf16[2,4096,4096]{2,1,0:T(8,128)(2,1)} %param.6), kind=kOutput, calls=%fused_computation.11 | convolution fusion | flops 4294967296 | bytes 14680064 | tf_op jit(solution)/shard_map/dot_general | solution.py:282
  248.9 6.9 %fusion.8 = f32[512,1024]{1,0:T(8,128)S(1)} fusion(bf16[512,4096]{1,0:T(8,128)(2,1)S(1)} %shard_map.59, bf16[2,4096,4096]{2,1,0:T(8,128)(2,1)} %param.6), kind=kOutput, calls=%fused_computation.9 | convolution fusion | flops 4294967296 | bytes 14680064 | tf_op jit(solution)/shard_map/dot_general | solution.py:282
  256.4 6.9 %fusion.6 = f32[512,1024]{1,0:T(8,128)S(1)} fusion(bf16[512,4096]{1,0:T(8,128)(2,1)S(1)} %shard_map.59, bf16[2,4096,4096]{2,1,0:T(8,128)(2,1)} %param.6), kind=kOutput, calls=%fused_computation.7 | convolution fusion | flops 4294967296 | bytes 14680064 | tf_op jit(solution)/shard_map/dot_general | solution.py:282
  265.8 2.4 maximum_select_fusion
  (67 shorter events, 16.6 us)
Async XLA Ops:
  0.6 16.7 %copy-start.2 = (bf16[256,4096]{1,0:T(8,128)(2,1)S(1)}, bf16[256,4096]{1,0:T(8,128)(2,1)}, u32[]{:S(2)}) copy-start(bf16[256,4096]{1,0:T(8,128)(2,1)} %param.4) | copy-start | bytes 6291460
  0.6 17.3 %collective-permute-start.1 = (bf16[256,4096]{1,0:T(8,128)(2,1)}, bf16[256,4096]{1,0:T(8,128)(2,1)}, u32[]{:S(2)}, u32[]{:S(2)}) collective-permute-start(bf16[256,4096]{1,0:T(8,128)(2,1)} %param.4), channel_id=1, source_target_pairs={{0,4},{4,0},{8,12},{12,8},{16,20},{20,16},{24,28},{28,24},{1,5},{5... | collective-permute-start | bytes 6291464 | tf_op jit(solution)/shard_map/ppermute | solution.py:19
  1.2 50.2 %collective-permute-start = (bf16[256,4096]{1,0:T(8,128)(2,1)}, bf16[256,4096]{1,0:T(8,128)(2,1)}, u32[]{:S(2)}, u32[]{:S(2)}) collective-permute-start(bf16[256,4096]{1,0:T(8,128)(2,1)} %param.4), channel_id=1, source_target_pairs={{0,8},{4,12},{8,16},{12,20},{16,24},{20,28},{1,9},{5,13},{9,17},{1... | collective-permute-start | bytes 6291464 | tf_op jit(solution)/shard_map/ppermute | solution.py:25
  16.3 1.0 copy-start
  22.5 29.0 %copy-start.3 = (bf16[128,4096]{1,0:T(8,128)(2,1)S(1)}, bf16[128,4096]{1,0:T(8,128)(2,1)}, u32[]{:S(2)}) copy-start(bf16[128,4096]{1,0:T(8,128)(2,1)} %param.7) | copy-start | bytes 3145732
  51.4 4.4 %collective-permute-start.2 = (bf16[256,4096]{1,0:T(8,128)(2,1)}, bf16[256,4096]{1,0:T(8,128)(2,1)S(1)}, u32[]{:S(2)}, u32[]{:S(2)}) collective-permute-start(bf16[256,4096]{1,0:T(8,128)(2,1)} %collective-permute-done), channel_id=1, source_target_pairs={{0,4},{4,0},{8,12},{12,8},{16,20},{20,16},{24,28},{28,24},{1,5},{5... | collective-permute-start | bytes 6291464 | tf_op jit(solution)/shard_map/ppermute | solution.py:19
  204.2 8.3 %collective-permute-start.3 = (bf16[256,1024]{1,0:T(8,128)(2,1)S(1)}, bf16[256,1024]{1,0:T(8,128)(2,1)S(1)}, u32[]{:S(2)}, u32[]{:S(2)}) collective-permute-start(bf16[256,1024]{1,0:T(8,128)(2,1)S(1)} %slice.223), channel_id=1, source_target_pairs={{0,4},{4,0},{8,12},{12,8},{16,20},{20,16},{24,28},{28,24},{1,5},{5... | collective-permute-start | bytes 1572872 | tf_op jit(solution)/shard_map/ppermute | solution.py:19
  212.6 9.1 %collective-permute-start.4 = (bf16[256,1024]{1,0:T(8,128)(2,1)S(1)}, bf16[256,1024]{1,0:T(8,128)(2,1)S(1)}, u32[]{:S(2)}, u32[]{:S(2)}) collective-permute-start(bf16[256,1024]{1,0:T(8,128)(2,1)S(1)} %slice.222), channel_id=1, source_target_pairs={{0,4},{4,0},{8,12},{12,8},{16,20},{20,16},{24,28},{28,24},{1,5},{5... | collective-permute-start | bytes 1572872 | tf_op jit(solution)/shard_map/ppermute | solution.py:19
  213.1 42.8 %collective-permute-start.8 = (bf16[256,1024]{1,0:T(8,128)(2,1)S(1)}, bf16[256,1024]{1,0:T(8,128)(2,1)S(1)}, u32[]{:S(2)}, u32[]{:S(2)}) collective-permute-start(bf16[256,1024]{1,0:T(8,128)(2,1)S(1)} %fusion.35), channel_id=1, source_target_pairs={{8,0},{12,4},{16,8},{20,12},{24,16},{28,20},{9,1},{13,5},{17,9},{2... | collective-permute-start | bytes 1572872 | tf_op jit(solution)/shard_map/ppermute | solution.py:25
  221.9 8.4 %collective-permute-start.5 = (bf16[256,1024]{1,0:T(8,128)(2,1)S(1)}, bf16[256,1024]{1,0:T(8,128)(2,1)S(1)}, u32[]{:S(2)}, u32[]{:S(2)}) collective-permute-start(bf16[256,1024]{1,0:T(8,128)(2,1)S(1)} %slice.221), channel_id=1, source_target_pairs={{0,4},{4,0},{8,12},{12,8},{16,20},{20,16},{24,28},{28,24},{1,5},{5... | collective-permute-start | bytes 1572872 | tf_op jit(solution)/shard_map/ppermute | solution.py:19
  222.0 42.1 %collective-permute-start.10 = (bf16[256,1024]{1,0:T(8,128)(2,1)S(1)}, bf16[256,1024]{1,0:T(8,128)(2,1)S(1)}, u32[]{:S(2)}, u32[]{:S(2)}) collective-permute-start(bf16[256,1024]{1,0:T(8,128)(2,1)S(1)} %fusion.34), channel_id=1, source_target_pairs={{8,0},{12,4},{16,8},{20,12},{24,16},{28,20},{9,1},{13,5},{17,9},{2... | collective-permute-start | bytes 1572872 | tf_op jit(solution)/shard_map/ppermute | solution.py:25
  230.4 8.9 %collective-permute-start.6 = (bf16[256,1024]{1,0:T(8,128)(2,1)S(1)}, bf16[256,1024]{1,0:T(8,128)(2,1)S(1)}, u32[]{:S(2)}, u32[]{:S(2)}) collective-permute-start(bf16[256,1024]{1,0:T(8,128)(2,1)S(1)} %slice.220), channel_id=1, source_target_pairs={{0,4},{4,0},{8,12},{12,8},{16,20},{20,16},{24,28},{28,24},{1,5},{5... | collective-permute-start | bytes 1572872 | tf_op jit(solution)/shard_map/ppermute | solution.py:19
  231.0 33.2 %collective-permute-start.12 = (bf16[256,1024]{1,0:T(8,128)(2,1)S(1)}, bf16[256,1024]{1,0:T(8,128)(2,1)S(1)}, u32[]{:S(2)}, u32[]{:S(2)}) collective-permute-start(bf16[256,1024]{1,0:T(8,128)(2,1)S(1)} %fusion.33), channel_id=1, source_target_pairs={{8,0},{12,4},{16,8},{20,12},{24,16},{28,20},{9,1},{13,5},{17,9},{2... | collective-permute-start | bytes 1572872 | tf_op jit(solution)/shard_map/ppermute | solution.py:25
  239.5 8.7 %collective-permute-start.7 = (bf16[256,1024]{1,0:T(8,128)(2,1)S(1)}, bf16[256,1024]{1,0:T(8,128)(2,1)S(1)}, u32[]{:S(2)}, u32[]{:S(2)}) collective-permute-start(bf16[256,1024]{1,0:T(8,128)(2,1)S(1)} %slice.219), channel_id=1, source_target_pairs={{0,4},{4,0},{8,12},{12,8},{16,20},{20,16},{24,28},{28,24},{1,5},{5... | collective-permute-start | bytes 1572872 | tf_op jit(solution)/shard_map/ppermute | solution.py:19
  239.6 24.9 %collective-permute-start.14 = (bf16[256,1024]{1,0:T(8,128)(2,1)S(1)}, bf16[256,1024]{1,0:T(8,128)(2,1)S(1)}, u32[]{:S(2)}, u32[]{:S(2)}) collective-permute-start(bf16[256,1024]{1,0:T(8,128)(2,1)S(1)} %fusion.32), channel_id=1, source_target_pairs={{8,0},{12,4},{16,8},{20,12},{24,16},{28,20},{9,1},{13,5},{17,9},{2... | collective-permute-start | bytes 1572872 | tf_op jit(solution)/shard_map/ppermute | solution.py:25
  248.4 7.8 %collective-permute-start.9 = (bf16[256,1024]{1,0:T(8,128)(2,1)S(1)}, bf16[256,1024]{1,0:T(8,128)(2,1)S(1)}, u32[]{:S(2)}, u32[]{:S(2)}) collective-permute-start(bf16[256,1024]{1,0:T(8,128)(2,1)S(1)} %slice.218), channel_id=1, source_target_pairs={{0,4},{4,0},{8,12},{12,8},{16,20},{20,16},{24,28},{28,24},{1,5},{5... | collective-permute-start | bytes 1572872 | tf_op jit(solution)/shard_map/ppermute | solution.py:19
  256.4 7.8 %collective-permute-start.11 = (bf16[256,1024]{1,0:T(8,128)(2,1)S(1)}, bf16[256,1024]{1,0:T(8,128)(2,1)S(1)}, u32[]{:S(2)}, u32[]{:S(2)}) collective-permute-start(bf16[256,1024]{1,0:T(8,128)(2,1)S(1)} %slice.217), channel_id=1, source_target_pairs={{0,4},{4,0},{8,12},{12,8},{16,20},{20,16},{24,28},{28,24},{1,5},{5... | collective-permute-start | bytes 1572872 | tf_op jit(solution)/shard_map/ppermute | solution.py:19
  263.5 2.3 copy-start.1
  263.5 2.1 collective-permute-start.13

commit v3 on v2

--- a/solution.py
+++ b/solution.py
@@ -244,6 +244,9 @@
 
     goal_place = 2 * (feat_pos // 2 != member) + feat_pos % 2
     own_part = jnp.dot(own_all, decoders[0], preferred_element_type=jnp.float32)
+    at_goal = jnp.arange(4)[:, None, None] == goal_place
+    goal = jnp.where(at_goal, targets.astype(jnp.float32)[None], 0.0)
+    own_part = own_part - goal.reshape(own_part.shape)
 
     raw_prior, own_part = tied(raw_before, own_part)
     prior_all = jnp.concatenate(
@@ -258,11 +261,8 @@
     def narrow(value):
         return value.astype(jnp.bfloat16)
 
-    goal = targets.astype(jnp.float32)
-    none = jnp.zeros_like(goal)
-    goal = jnp.concatenate([jnp.where(goal_place == p, goal, none) for p in range(4)], 0)
     partial = own_part + jnp.dot(prior_all, decoders[1], preferred_element_type=jnp.float32)
-    errors = summed_on_line(partial - goal)
+    errors = summed_on_line(partial)
 
     jobs = [(span, p) for span in (1, 0) for p in range(PARTS)]
     held_terms, given, sums = [], [], []

time: 273 us -> 278 us (1.018); the launches traced: 268 us -> 277 us
  other arithmetic: 21.7 us -> 28.5 us
    add x0 -> x1, other arithmetic: none -> 11.1 us  [chain_local(): own_part + jnp.dot(prior_all, decoders[1], preferred_element_type=jnp.flo...]
    sub x1 -> x0, other arithmetic: 9.22 us -> none  [chain_local(): errors = summed_on_line(partial - goal)]
    select_n x5, other arithmetic: 7.24 us -> 10.5 us  [masked(): return jnp.where(mask, rows, jnp.zeros_like(rows))]
  transfers between devices with their start and end apart: 15 -> 15, of which waited for: 3 -> 2; matrix products, arithmetic and copies ran while one was open for 34% -> 35% of each run, Pallas kernels for 0% -> 0%
where the time goes in v3:
time: 278 us; the launch traced here: 277 us
  Pallas kernels  108 us (39%)
  matrix products  102 us (37%)
  other arithmetic  28.5 us (10%)
  local copies, waits for them, and re-layouts  14.5 us (5%)
  starting transfers between devices  14.4 us (5%)
  waiting for transfers between devices  8.39 us (3%)
    pallas_call x1, Pallas kernels, summed_on_line(): pl.pallas_call(functools.partial(line_kernel, CHUNKS), out_shape=jax.Shap...  108 us
    dot_general x8, matrix products, chain_local(): lax.dot_general(rows, decoders[span, part * size:(part + 1) * size], (((1...  55.5 us
    dot_general x1, matrix products, chain_local(): jnp.dot(prior_all, decoders[1], preferred_element_type=jnp.float32)  23.3 us
    dot_general x1, matrix products, chain_local(): own_part = jnp.dot(own_all, decoders[0], preferred_element_type=jnp.float32)  23.1 us
    ppermute x5, starting transfers between devices, passed_along(): lax.ppermute(value, axis, [(source, source + steps) for source in range(f...  11.2 us
    add x1, other arithmetic, chain_local(): own_part + jnp.dot(prior_all, decoders[1], preferred_element_type=jnp.flo...  11.1 us
    select_n x5, other arithmetic, masked(): return jnp.where(mask, rows, jnp.zeros_like(rows))  10.5 us
    broadcast_in_dim x8, local copies, waits for them, and re-layouts, mask_of(): return jnp.repeat(jnp.repeat(hit, block_rows, axis=0), BLOCK, axis=1)  8.29 us
  transfers between devices with their start and end apart: 15, of which 2 were waited for; matrix products, arithmetic and copies ran while one was open for 35% of the time, Pallas kernels for 0%

profile of v3, /device:TPU:0, one launch (start us, length us, event | category | flops | bytes accessed | tf_op | source)
XLA Modules:
  0.0 277.1 jit_solution(14233539163155779916)
XLA Ops:
  1.1 5.8 %collective-permute-start = (bf16[256,4096]{1,0:T(8,128)(2,1)}, bf16[256,4096]{1,0:T(8,128)(2,1)}, u32[]{:S(2)}, u32[]{:S(2)}) collective-permute-start(bf16[256,4096]{1,0:T(8,128)(2,1)} %param.4), channel_id=1, source_target_pairs={{0,8},{4,12},{8,16},{12,20},{16,24},{20,28},{1,9},{5,13},{9,17},{1... | collective-permute-start | bytes 6291464 | tf_op jit(solution)/shard_map/ppermute | solution.py:25
  8.4 2.1 broadcast_in_dim.64
  11.5 2.2 bitcast_select_fusion.2
  13.7 2.1 broadcast_in_dim.68
  16.5 2.1 broadcast_in_dim.70
  20.3 2.8 convert_element_type.60
  23.2 2.1 broadcast_in_dim.66
  25.2 2.2 bitcast_select_fusion.1
  29.0 23.1 %fusion.22 = f32[512,4096]{1,0:T(8,128)} fusion(bf16[512,4096]{1,0:T(8,128)(2,1)S(1)} %pad_maximum_fusion, bf16[2,4096,4096]{2,1,0:T(8,128)(2,1)} %param.6, f32[128,4096]{1,0:T(8,128)S(1)} %copy-done.3, pred[512]{0:T(512)(128)(4,1)S(1)} %broadcast_bitcast_fusion), kind=kOutput, calls=%fused_computation.23 | convolution fusion | flops 17184063488 | bytes 48235008 | tf_op jit(solution)/shard_map/dot_general | solution.py:246
  52.3 1.9 broadcast_select_fusion.1
  54.2 2.4 collective-permute-done.2
  58.7 23.3 %fusion = f32[512,4096]{1,0:T(8,128)} fusion(bf16[512,4096]{1,0:T(8,128)(2,1)S(1)} %pad_maximum_fusion.1, bf16[2,4096,4096]{2,1,0:T(8,128)(2,1)} %param.6), kind=kOutput, calls=%fused_computation | convolution fusion | flops 17179869184 | bytes 46137344 | tf_op jit(solution)/shard_map/dot_general | solution.py:264
  81.9 11.1 %add.85.partial = f32[512,4096]{1,0:T(8,128)} add(f32[512,4096]{1,0:T(8,128)} %fusion.22, f32[512,4096]{1,0:T(8,128)} %fusion) | non-fusion elementwise | flops 2097152 | bytes 25165824 | tf_op jit(solution)/shard_map/add | solution.py:264
  93.1 108.3 %shard_map.59 = bf16[512,4096]{1,0:T(8,128)(2,1)S(1)} custom-call(f32[512,4096]{1,0:T(8,128)} %add.85.partial), custom_call_target="tpu_custom_call" | custom-call | flops 8388608 | bytes 12582912 | tf_op jit(solution)/shard_map/pallas_call | solution.py:190
  201.4 6.9 %fusion.20 = f32[512,1024]{1,0:T(8,128)S(1)} fusion(bf16[512,4096]{1,0:T(8,128)(2,1)S(1)} %shard_map.59, bf16[2,4096,4096]{2,1,0:T(8,128)(2,1)} %param.6), kind=kOutput, calls=%fused_computation.20 | convolution fusion | flops 4294967296 | bytes 14680064 | tf_op jit(solution)/shard_map/dot_general | solution.py:282
  208.5 7.0 %fusion.18 = f32[512,1024]{1,0:T(8,128)S(1)} fusion(bf16[512,4096]{1,0:T(8,128)(2,1)S(1)} %shard_map.59, bf16[2,4096,4096]{2,1,0:T(8,128)(2,1)} %param.6), kind=kOutput, calls=%fused_computation.18 | convolution fusion | flops 4294967296 | bytes 14680064 | tf_op jit(solution)/shard_map/dot_general | solution.py:282
  217.4 6.9 %fusion.16 = f32[512,1024]{1,0:T(8,128)S(1)} fusion(bf16[512,4096]{1,0:T(8,128)(2,1)S(1)} %shard_map.59, bf16[2,4096,4096]{2,1,0:T(8,128)(2,1)} %param.6), kind=kOutput, calls=%fused_computation.16 | convolution fusion | flops 4294967296 | bytes 14680064 | tf_op jit(solution)/shard_map/dot_general | solution.py:282
  226.0 6.9 %fusion.14 = f32[512,1024]{1,0:T(8,128)S(1)} fusion(bf16[512,4096]{1,0:T(8,128)(2,1)S(1)} %shard_map.59, bf16[2,4096,4096]{2,1,0:T(8,128)(2,1)} %param.6), kind=kOutput, calls=%fused_computation.14 | convolution fusion | flops 4294967296 | bytes 14680064 | tf_op jit(solution)/shard_map/dot_general | solution.py:282
  235.1 6.9 %fusion.12 = f32[512,1024]{1,0:T(8,128)S(1)} fusion(bf16[512,4096]{1,0:T(8,128)(2,1)S(1)} %shard_map.59, bf16[2,4096,4096]{2,1,0:T(8,128)(2,1)} %param.6), kind=kOutput, calls=%fused_computation.12 | convolution fusion | flops 4294967296 | bytes 14680064 | tf_op jit(solution)/shard_map/dot_general | solution.py:282
  243.9 6.9 %fusion.10 = f32[512,1024]{1,0:T(8,128)S(1)} fusion(bf16[512,4096]{1,0:T(8,128)(2,1)S(1)} %shard_map.59, bf16[2,4096,4096]{2,1,0:T(8,128)(2,1)} %param.6), kind=kOutput, calls=%fused_computation.10 | convolution fusion | flops 4294967296 | bytes 14680064 | tf_op jit(solution)/shard_map/dot_general | solution.py:282
  253.0 6.9 %fusion.8 = f32[512,1024]{1,0:T(8,128)S(1)} fusion(bf16[512,4096]{1,0:T(8,128)(2,1)S(1)} %shard_map.59, bf16[2,4096,4096]{2,1,0:T(8,128)(2,1)} %param.6), kind=kOutput, calls=%fused_computation.8 | convolution fusion | flops 4294967296 | bytes 14680064 | tf_op jit(solution)/shard_map/dot_general | solution.py:282
  260.2 7.0 %fusion.6 = f32[512,1024]{1,0:T(8,128)S(1)} fusion(bf16[512,4096]{1,0:T(8,128)(2,1)S(1)} %shard_map.59, bf16[2,4096,4096]{2,1,0:T(8,128)(2,1)} %param.6), kind=kOutput, calls=%fused_computation.6 | convolution fusion | flops 4294967296 | bytes 14680064 | tf_op jit(solution)/shard_map/dot_general | solution.py:282
  268.2 6.0 %collective-permute-done.14 = bf16[256,1024]{1,0:T(8,128)(2,1)S(1)} collective-permute-done((bf16[256,1024]{1,0:T(8,128)(2,1)S(1)}, bf16[256,1024]{1,0:T(8,128)(2,1)S(1)}, u32[]{:S(2)}, u32[]{:S(2)}) %collective-permute-start.14) | collective-permute-done | bytes 524320 | tf_op jit(solution)/shard_map/ppermute | solution.py:25
  274.7 2.4 maximum_select_fusion
  (69 shorter events, 20.9 us)
Async XLA Ops:
  0.6 22.5 %collective-permute-start.1 = (bf16[256,4096]{1,0:T(8,128)(2,1)}, bf16[256,4096]{1,0:T(8,128)(2,1)}, u32[]{:S(2)}, u32[]{:S(2)}) collective-permute-start(bf16[256,4096]{1,0:T(8,128)(2,1)} %param.4), channel_id=1, source_target_pairs={{0,4},{4,0},{8,12},{12,8},{16,20},{20,16},{24,28},{28,24},{1,5},{5... | collective-permute-start | bytes 6291464 | tf_op jit(solution)/shard_map/ppermute | solution.py:19
  1.1 50.9 %collective-permute-start = (bf16[256,4096]{1,0:T(8,128)(2,1)}, bf16[256,4096]{1,0:T(8,128)(2,1)}, u32[]{:S(2)}, u32[]{:S(2)}) collective-permute-start(bf16[256,4096]{1,0:T(8,128)(2,1)} %param.4), channel_id=1, source_target_pairs={{0,8},{4,12},{8,16},{12,20},{16,24},{20,28},{1,9},{5,13},{9,17},{1... | collective-permute-start | bytes 6291464 | tf_op jit(solution)/shard_map/ppermute | solution.py:25
  10.5 1.0 copy-start
  27.4 1.6 copy-start.3
  52.1 4.5 %copy-start.2 = (pred[32,8,32,128]{3,1,2,0:T(8,128)(4,1)S(1)}, pred[32,8,32,128]{3,1,2,0:T(8,128)(4,1)}, u32[]{:S(2)}) copy-start(pred[32,8,32,128]{3,1,2,0:T(8,128)(4,1)} %copy.15) | copy-start | bytes 3145732
  52.1 4.5 %collective-permute-start.2 = (bf16[256,4096]{1,0:T(8,128)(2,1)}, bf16[256,4096]{1,0:T(8,128)(2,1)}, u32[]{:S(2)}, u32[]{:S(2)}) collective-permute-start(bf16[256,4096]{1,0:T(8,128)(2,1)} %collective-permute-done), channel_id=1, source_target_pairs={{0,4},{4,0},{8,12},{12,8},{16,20},{20,16},{24,28},{28,24},{1,5},{5... | collective-permute-start | bytes 6291464 | tf_op jit(solution)/shard_map/ppermute | solution.py:19
  208.4 8.3 %collective-permute-start.3 = (bf16[256,1024]{1,0:T(8,128)(2,1)S(1)}, bf16[256,1024]{1,0:T(8,128)(2,1)S(1)}, u32[]{:S(2)}, u32[]{:S(2)}) collective-permute-start(bf16[256,1024]{1,0:T(8,128)(2,1)S(1)} %slice.225), channel_id=1, source_target_pairs={{0,4},{4,0},{8,12},{12,8},{16,20},{20,16},{24,28},{28,24},{1,5},{5... | collective-permute-start | bytes 1572872 | tf_op jit(solution)/shard_map/ppermute | solution.py:19
  216.9 8.9 %collective-permute-start.4 = (bf16[256,1024]{1,0:T(8,128)(2,1)S(1)}, bf16[256,1024]{1,0:T(8,128)(2,1)S(1)}, u32[]{:S(2)}, u32[]{:S(2)}) collective-permute-start(bf16[256,1024]{1,0:T(8,128)(2,1)S(1)} %slice.224), channel_id=1, source_target_pairs={{0,4},{4,0},{8,12},{12,8},{16,20},{20,16},{24,28},{28,24},{1,5},{5... | collective-permute-start | bytes 1572872 | tf_op jit(solution)/shard_map/ppermute | solution.py:19
  224.4 42.9 %collective-permute-start.8 = (bf16[256,1024]{1,0:T(8,128)(2,1)S(1)}, bf16[256,1024]{1,0:T(8,128)(2,1)S(1)}, u32[]{:S(2)}, u32[]{:S(2)}) collective-permute-start(bf16[256,1024]{1,0:T(8,128)(2,1)S(1)} %fusion.38), channel_id=1, source_target_pairs={{8,0},{12,4},{16,8},{20,12},{24,16},{28,20},{9,1},{13,5},{17,9},{2... | collective-permute-start | bytes 1572872 | tf_op jit(solution)/shard_map/ppermute | solution.py:25
  225.9 8.4 %collective-permute-start.5 = (bf16[256,1024]{1,0:T(8,128)(2,1)S(1)}, bf16[256,1024]{1,0:T(8,128)(2,1)S(1)}, u32[]{:S(2)}, u32[]{:S(2)}) collective-permute-start(bf16[256,1024]{1,0:T(8,128)(2,1)S(1)} %slice.223), channel_id=1, source_target_pairs={{0,4},{4,0},{8,12},{12,8},{16,20},{20,16},{24,28},{28,24},{1,5},{5... | collective-permute-start | bytes 1572872 | tf_op jit(solution)/shard_map/ppermute | solution.py:19
  233.0 35.0 %collective-permute-start.10 = (bf16[256,1024]{1,0:T(8,128)(2,1)S(1)}, bf16[256,1024]{1,0:T(8,128)(2,1)S(1)}, u32[]{:S(2)}, u32[]{:S(2)}) collective-permute-start(bf16[256,1024]{1,0:T(8,128)(2,1)S(1)} %fusion.37), channel_id=1, source_target_pairs={{8,0},{12,4},{16,8},{20,12},{24,16},{28,20},{9,1},{13,5},{17,9},{2... | collective-permute-start | bytes 1572872 | tf_op jit(solution)/shard_map/ppermute | solution.py:25
  234.5 9.1 %collective-permute-start.6 = (bf16[256,1024]{1,0:T(8,128)(2,1)S(1)}, bf16[256,1024]{1,0:T(8,128)(2,1)S(1)}, u32[]{:S(2)}, u32[]{:S(2)}) collective-permute-start(bf16[256,1024]{1,0:T(8,128)(2,1)S(1)} %slice.222), channel_id=1, source_target_pairs={{0,4},{4,0},{8,12},{12,8},{16,20},{20,16},{24,28},{28,24},{1,5},{5... | collective-permute-start | bytes 1572872 | tf_op jit(solution)/shard_map/ppermute | solution.py:19
  242.1 32.3 %collective-permute-start.12 = (bf16[256,1024]{1,0:T(8,128)(2,1)S(1)}, bf16[256,1024]{1,0:T(8,128)(2,1)S(1)}, u32[]{:S(2)}, u32[]{:S(2)}) collective-permute-start(bf16[256,1024]{1,0:T(8,128)(2,1)S(1)} %fusion.36), channel_id=1, source_target_pairs={{8,0},{12,4},{16,8},{20,12},{24,16},{28,20},{9,1},{13,5},{17,9},{2... | collective-permute-start | bytes 1572872 | tf_op jit(solution)/shard_map/ppermute | solution.py:25
  243.8 8.4 %collective-permute-start.7 = (bf16[256,1024]{1,0:T(8,128)(2,1)S(1)}, bf16[256,1024]{1,0:T(8,128)(2,1)S(1)}, u32[]{:S(2)}, u32[]{:S(2)}) collective-permute-start(bf16[256,1024]{1,0:T(8,128)(2,1)S(1)} %slice.221), channel_id=1, source_target_pairs={{0,4},{4,0},{8,12},{12,8},{16,20},{20,16},{24,28},{28,24},{1,5},{5... | collective-permute-start | bytes 1572872 | tf_op jit(solution)/shard_map/ppermute | solution.py:19
  250.9 23.2 %collective-permute-start.14 = (bf16[256,1024]{1,0:T(8,128)(2,1)S(1)}, bf16[256,1024]{1,0:T(8,128)(2,1)S(1)}, u32[]{:S(2)}, u32[]{:S(2)}) collective-permute-start(bf16[256,1024]{1,0:T(8,128)(2,1)S(1)} %fusion.35), channel_id=1, source_target_pairs={{8,0},{12,4},{16,8},{20,12},{24,16},{28,20},{9,1},{13,5},{17,9},{2... | collective-permute-start | bytes 1572872 | tf_op jit(solution)/shard_map/ppermute | solution.py:25
  252.4 7.6 %collective-permute-start.9 = (bf16[256,1024]{1,0:T(8,128)(2,1)S(1)}, bf16[256,1024]{1,0:T(8,128)(2,1)S(1)}, u32[]{:S(2)}, u32[]{:S(2)}) collective-permute-start(bf16[256,1024]{1,0:T(8,128)(2,1)S(1)} %slice.220), channel_id=1, source_target_pairs={{0,4},{4,0},{8,12},{12,8},{16,20},{20,16},{24,28},{28,24},{1,5},{5... | collective-permute-start | bytes 1572872 | tf_op jit(solution)/shard_map/ppermute | solution.py:19
  267.2 6.9 %collective-permute-start.13 = (bf16[256,1024]{1,0:T(8,128)(2,1)S(1)}, bf16[256,1024]{1,0:T(8,128)(2,1)S(1)}, u32[]{:S(2)}, u32[]{:S(2)}) collective-permute-start(bf16[256,1024]{1,0:T(8,128)(2,1)S(1)} %slice.218), channel_id=1, source_target_pairs={{0,4},{4,0},{8,12},{12,8},{16,20},{20,16},{24,28},{28,24},{1,5},{5... | collective-permute-start | bytes 1572872 | tf_op jit(solution)/shard_map/ppermute | solution.py:19
  267.5 7.2 %copy-start.1 = (pred[256,32,128]{2,1,0:T(8,128)(4,1)S(1)}, pred[256,32,128]{2,1,0:T(8,128)(4,1)}, u32[]{:S(2)}) copy-start(pred[256,32,128]{2,1,0:T(8,128)(4,1)} %copy-done) | copy-start | bytes 3145732
  267.5 6.9 %collective-permute-start.11 = (bf16[256,1024]{1,0:T(8,128)(2,1)S(1)}, bf16[256,1024]{1,0:T(8,128)(2,1)S(1)}, u32[]{:S(2)}, u32[]{:S(2)}) collective-permute-start(bf16[256,1024]{1,0:T(8,128)(2,1)S(1)} %slice.219), channel_id=1, source_target_pairs={{0,4},{4,0},{8,12},{12,8},{16,20},{20,16},{24,28},{28,24},{1,5},{5... | collective-permute-start | bytes 1572872 | tf_op jit(solution)/shard_map/ppermute | solution.py:19
